TPU v7x, 128 devices: a whole 4x4x4 slice. The times are simulated.
128 devices in a mesh: slab: 32 (over z, y, core), chan: 4 (over x).
Axes of the slice: x: 4, y: 4, z: 4, core: 2. Of those that a mesh axis runs over, the one named last changes fastest.
Arguments:
- field: bfloat16 [64, 64, 128, 512], P('slab', None, 'chan'), may hold values from -8 to 8
- spectral_weights: float32 [2, 64, 8, 8, 128, 128], P(None, 'slab', None, None, 'chan'), may hold values from -0.5 to 0.5
- bias: float32 [128], P('chan'), may hold values from -3 to 3
Outputs:
- updated: float32 [64, 64, 128, 512], P('slab', None, 'chan')
All inputs are finite; a program needn't handle non-finite values.
Results may differ from a plain program's by a relative error of at most 0.0003.
Values sent between devices are 32-bit elements; how exact they have to be, the bound alone decides.
A program may use at most 128 MiB of HBM per device.

v0:
```python
import functools
import math

import jax
import jax.numpy as jnp
import ml_dtypes
import numpy as np
from jax import lax
from jax.experimental import pallas as pl
from jax.experimental.pallas import tpu as pltpu
from jax.sharding import PartitionSpec as P

GX, GY, GZ, GT = 64, 64, 32, 16
MX, MY, MT = 8, 8, 8
KQ, ZT = 64, 512
SLABS, CHANS = 32, 4
XL = GX // SLABS
QL = KQ // SLABS
CL = 32
LANES = 128
BLOCK = 16
MESH = pl.DeviceIdType.MESH
MIB = 1 << 20

GELU_Q = (
    7.97884216e-01,
    3.63342835e-02,
    -3.31299940e-05,
    -5.52401584e-05,
    3.96910946e-06,
    -1.33446409e-07,
    1.80561642e-09,
)
GELU_H = tuple(c * 2.0 * 4.0**k for k, c in enumerate(GELU_Q))


def split_bf16(table):
    high = table.astype(np.float32).astype(ml_dtypes.bfloat16)
    low = (table - high.astype(np.float64)).astype(np.float32).astype(ml_dtypes.bfloat16)
    return high, low


def zt_angles():
    cells = np.arange(ZT)[:, None]
    lanes = np.arange(KQ)[None, :]
    modes = (lanes % SLABS) * QL + lanes // SLABS
    counted = (modes // MT) * (cells // GT) % GZ * GT + (modes % MT) * (cells % GT) % GT * GZ
    return 2.0 * math.pi * counted / (GZ * GT), modes


def forward_zt_table():
    angles, _ = zt_angles()
    high, low = split_bf16(np.concatenate([np.cos(angles), -np.sin(angles)], axis=1))
    return np.concatenate([high, low], axis=1)


def inverse_zt_table():
    angles, modes = zt_angles()
    weight = np.where(modes % MT == 0, 1.0, 2.0) / (GX * GY * GZ * GT) / 2.0
    table = np.concatenate([weight * np.cos(angles), -weight * np.sin(angles)], axis=1).T
    high, low = split_bf16(table)
    return np.concatenate([high, high, low], axis=0)


def forward_x_table():
    angles = 2.0 * math.pi * (np.arange(MX)[:, None] * np.arange(GX)[None, :] % GX) / GX
    cos, sin = np.cos(angles), np.sin(angles)
    real = np.concatenate([cos, sin], axis=1)
    imag = np.concatenate([-sin, cos], axis=1)
    return np.stack([real, imag], axis=1).reshape(2 * MX, 2 * GX).astype(np.float32)


def inverse_x_table():
    angles = 2.0 * math.pi * (np.arange(GX)[:, None] * np.arange(MX)[None, :] % GX) / GX
    cos, sin = np.cos(angles), np.sin(angles)
    real = np.stack([cos, -sin], axis=2).reshape(GX, 2 * MX)
    imag = np.stack([sin, cos], axis=2).reshape(GX, 2 * MX)
    return np.concatenate([real, imag], axis=0).astype(np.float32)


def cos_y(k, y):
    return math.cos(2.0 * math.pi * (k * y % GY) / GY)


def sin_y(k, y):
    return math.sin(2.0 * math.pi * (k * y % GY) / GY)


def dot(a, b, precision=None):
    return jnp.dot(a, b, preferred_element_type=jnp.float32, precision=precision)


def total(terms):
    terms = list(terms)
    while len(terms) > 1:
        terms = [
            terms[i] + terms[i + 1] if i + 1 < len(terms) else terms[i]
            for i in range(0, len(terms), 2)
        ]
    return terms[0]


def rotate_parts(values, sign):
    lane = lax.broadcasted_iota(jnp.int32, values.shape, values.ndim - 1)
    swapped = pltpu.roll(values, LANES // 2, values.ndim - 1)
    return jnp.where(lane < LANES // 2, sign, -sign) * swapped


def forward_kernel(field_ref, table_ref, out_ref, modes_ref, kept_ref):
    plane, chunk = pl.program_id(0), pl.program_id(1)
    chunks = pl.num_programs(1)
    rows_y = field_ref.shape[1]
    both = dot(field_ref[...].reshape(rows_y * CL, ZT), table_ref[...])
    modes_ref[pl.ds(chunk * rows_y, rows_y)] = (both[:, :LANES] + both[:, LANES:]).reshape(
        rows_y, CL, LANES
    )

    @pl.when(chunk == chunks - 1)
    def _():
        half = GY // 2
        for group in range(CL // 8):
            rows = pl.ds(group * 8, 8)

            def load(y):
                return modes_ref[y, rows, :]

            first, middle = load(0), load(half)
            even, odd = first + middle, first - middle
            cosines = [even if k % 2 == 0 else odd for k in range(MY)]
            first, middle = load(half // 2), load(half // 2 + half)
            even, odd = first + middle, first - middle
            sines = [None] * MY
            for k in range(MY):
                if k % 2 == 0:
                    cosines[k] = cosines[k] + (even if k % 4 == 0 else -even)
                else:
                    sines[k] = odd if k % 4 == 1 else -odd
            for y in range(1, half // 2):
                a, b, c, d = load(y), load(GY - y), load(half - y), load(half + y)
                sum1, dif1, sum2, dif2 = a + b, a - b, c + d, c - d
                for_even, for_odd = sum1 + sum2, sum1 - sum2
                sin_odd, sin_even = dif1 + dif2, dif1 - dif2
                for k in range(MY):
                    cosines[k] = cosines[k] + cos_y(k, y) * (for_even if k % 2 == 0 else for_odd)
                    if k > 0:
                        term = sin_y(k, y) * (sin_even if k % 2 == 0 else sin_odd)
                        sines[k] = term if sines[k] is None else sines[k] + term
            for k in range(MY):
                value = cosines[k]
                if k > 0:
                    value = value + rotate_parts(sines[k], 1.0)
                kept_ref[pl.ds(k * CL + group * 8, 8), :] = value
        for ky_half in range(2):
            turned = kept_ref[pl.ds(ky_half * LANES, LANES), :].T
            for part in range(4):
                for owners in range(SLABS // 8):
                    start = owners * 8 * BLOCK + plane * 8 + ky_half * 4 + part
                    out_ref[pl.ds(start, 8, stride=BLOCK), :] = turned[
                        part * SLABS + owners * 8 : part * SLABS + owners * 8 + 8
                    ]


def forward(field, table):
    rows_y = 16
    return pl.pallas_call(
        forward_kernel,
        grid=(XL, GY // rows_y),
        in_specs=[
            pl.BlockSpec((1, rows_y, CL, ZT), lambda x, y: (x, y, 0, 0)),
            pl.BlockSpec((ZT, 2 * LANES), lambda x, y: (0, 0)),
        ],
        out_specs=pl.BlockSpec((SLABS * BLOCK, LANES), lambda x, y: (0, 0)),
        out_shape=jax.ShapeDtypeStruct((SLABS * BLOCK, LANES), jnp.float32),
        scratch_shapes=[
            pltpu.VMEM((GY, CL, LANES), jnp.float32),
            pltpu.VMEM((MY * CL, LANES), jnp.float32),
        ],
        compiler_params=pltpu.CompilerParams(vmem_limit_bytes=32 * MIB),
    )(field, table)


def exchange_kernel(
    ready_ref,
    weights_ref,
    x_forward_ref,
    x_inverse_ref,
    out_ref,
    arrived,
    staged,
    high_ref,
    low_ref,
    spectrum_ref,
    partial_ref,
    parcels,
    parcels_in,
    outgoing,
    weight_sem,
    local_sem,
    send_sem,
    recv_sem,
    chan_send,
    chan_recv,
    back_send,
    back_recv,
):
    slab, chan = lax.axis_index("slab"), lax.axis_index("chan")
    highest = lax.Precision.HIGHEST

    def weight_copy(part):
        return pltpu.make_async_copy(weights_ref.at[part], staged.at[part], weight_sem.at[part])

    for part in range(2):
        weight_copy(part).start()

    barrier = pltpu.get_barrier_semaphore()

    def greet_slab(i, carry):
        pl.semaphore_signal(
            barrier, inc=1, device_id=(lax.rem(slab + i, SLABS), chan), device_id_type=MESH
        )
        return carry

    def greet_chan(i, carry):
        pl.semaphore_signal(
            barrier, inc=1, device_id=(slab, lax.rem(chan + i, CHANS)), device_id_type=MESH
        )
        return carry

    lax.fori_loop(1, SLABS, greet_slab, 0)
    lax.fori_loop(1, CHANS, greet_chan, 0)
    pl.semaphore_wait(barrier, SLABS + CHANS - 2)

    def block_of(owner):
        return pl.ds(pl.multiple_of(owner * BLOCK, BLOCK), BLOCK)

    def send_all(source, target, send, recv):
        def step(i, carry):
            other = lax.rem(slab + i, SLABS)
            pltpu.make_async_remote_copy(
                src_ref=source.at[block_of(other)],
                dst_ref=target.at[block_of(slab)],
                send_sem=send,
                recv_sem=recv,
                device_id=(other, chan),
                device_id_type=MESH,
            ).start()
            return carry

        lax.fori_loop(1, SLABS, step, 0)
        own = pltpu.make_async_copy(
            source.at[block_of(slab)], target.at[block_of(slab)], local_sem
        )
        own.start()
        return own

    def wait_bytes(ref, rows, sem):
        piece = ref.at[pl.ds(0, rows)]
        pltpu.make_async_copy(piece, piece, sem).wait()

    own = send_all(ready_ref, arrived, send_sem, recv_sem)

    for part in range(2):
        weight_copy(part).wait()

        def split_weights(i, carry, part=part):
            value = staged[part, i]
            high = value.astype(jnp.bfloat16)
            low = (value - high.astype(jnp.float32)).astype(jnp.bfloat16)
            high_ref[i, :, part * LANES : (part + 1) * LANES] = high
            low_ref[i, :, part * LANES : (part + 1) * LANES] = low
            return carry

        lax.fori_loop(0, QL * MX, split_weights, 0)

    own.wait()
    rows_sent = (SLABS - 1) * BLOCK
    wait_bytes(arrived, rows_sent, recv_sem)

    columns = []
    for parity in range(QL):
        for ky_half in range(2):
            columns.append(
                jnp.concatenate(
                    [
                        arrived[pl.ds(ky_half * 4 + part * 2 + parity, GX, stride=8), :]
                        for part in range(2)
                    ],
                    axis=0,
                )
            )
    spectrum = dot(x_forward_ref[...], jnp.concatenate(columns, axis=1), highest)
    for parity in range(QL):
        spectrum_ref[parity] = spectrum[:, parity * 256 : (parity + 1) * 256]

    row = lax.broadcasted_iota(jnp.int32, (MY, 256), 0)
    lane = lax.broadcasted_iota(jnp.int32, (MY, 256), 1)
    own_ky = row == lane // CL

    def mix(parity, carry):
        for kx in range(MX):
            spread = jnp.concatenate(
                [
                    jnp.where(own_ky, spectrum_ref[parity, pl.ds(2 * kx + part, 1), :], 0.0)
                    for part in range(2)
                ],
                axis=0,
            )
            high = spread.astype(jnp.bfloat16)
            low = (spread - high.astype(jnp.float32)).astype(jnp.bfloat16)
            main = dot(jnp.concatenate([high, low], axis=0), high_ref[parity * MX + kx])
            rest = dot(high, low_ref[parity * MX + kx])
            both = main[:16] + main[16:] + rest
            real = both[:8, :LANES] - both[8:, LANES:]
            imag = both[:8, LANES:] + both[8:, :LANES]
            partial_ref[pl.ds(parity * LANES + kx * 16, 8), :] = real
            partial_ref[pl.ds(parity * LANES + kx * 16 + 8, 8), :] = imag
        return carry

    lax.fori_loop(0, QL, mix, 0)

    lane = lax.broadcasted_iota(jnp.int32, (8, LANES), 1) // CL
    for parity in range(QL):
        for ky_half in range(2):
            for rows in range(2):
                pieces = [
                    partial_ref[
                        pl.ds(parity * LANES + rows * 64 + ky_half * 4 + ky, 8, stride=8), :
                    ]
                    for ky in range(4)
                ]
                for other in range(CHANS):
                    packed = None
                    for ky in range(4):
                        shift = (ky - other) % CHANS * CL
                        moved = pltpu.roll(pieces[ky], shift, 1) if shift else pieces[ky]
                        packed = moved if packed is None else jnp.where(lane == ky, moved, packed)
                    start = (parity * 2 + ky_half) * 16 + rows * 8
                    parcels[other, pl.ds(start, 8), :] = packed

    chan_copies = []
    for i in range(1, CHANS):
        other = lax.rem(chan + i, CHANS)
        copy = pltpu.make_async_remote_copy(
            src_ref=parcels.at[other],
            dst_ref=parcels_in.at[i - 1],
            send_sem=chan_send.at[i - 1],
            recv_sem=chan_recv.at[i - 1],
            device_id=(slab, other),
            device_id_type=MESH,
        )
        copy.start()
        chan_copies.append(copy)
    mixed = parcels[chan]
    for i in range(1, CHANS):
        chan_copies[i - 1].wait_recv()
        mixed = mixed + parcels_in[i - 1]

    side = jnp.concatenate([mixed[16 * i : 16 * i + 16] for i in range(4)], axis=1)
    spatial = dot(x_inverse_ref[...], side, highest)
    for parity in range(QL):
        for ky_half in range(2):
            for part in range(2):
                at = parity * 2 + ky_half
                outgoing[pl.ds(ky_half * 4 + part * 2 + parity, GX, stride=8), :] = spatial[
                    part * GX : (part + 1) * GX, at * LANES : (at + 1) * LANES
                ]

    own = send_all(outgoing, out_ref, back_send, back_recv)
    own.wait()
    for copy in chan_copies:
        copy.wait_send()
    wait_bytes(ready_ref, rows_sent, send_sem)
    wait_bytes(out_ref, rows_sent, back_recv)
    wait_bytes(outgoing, rows_sent, back_send)


def exchange(ready, weights, x_forward, x_inverse):
    vmem = pl.BlockSpec(memory_space=pltpu.VMEM)
    rows = SLABS * BLOCK
    return pl.pallas_call(
        exchange_kernel,
        in_specs=[vmem, pl.BlockSpec(memory_space=pl.ANY), vmem, vmem],
        out_specs=vmem,
        out_shape=jax.ShapeDtypeStruct((rows, LANES), jnp.float32),
        scratch_shapes=[
            pltpu.VMEM((rows, LANES), jnp.float32),
            pltpu.VMEM((2, QL * MX, 256, LANES), jnp.float32),
            pltpu.VMEM((QL * MX, 256, 256), jnp.bfloat16),
            pltpu.VMEM((QL * MX, 256, 256), jnp.bfloat16),
            pltpu.VMEM((QL, 16, 256), jnp.float32),
            pltpu.VMEM((QL * LANES, LANES), jnp.float32),
            pltpu.VMEM((CHANS, 64, LANES), jnp.float32),
            pltpu.VMEM((CHANS - 1, 64, LANES), jnp.float32),
            pltpu.VMEM((rows, LANES), jnp.float32),
            pltpu.SemaphoreType.DMA((2,)),
            pltpu.SemaphoreType.DMA,
            pltpu.SemaphoreType.DMA,
            pltpu.SemaphoreType.DMA,
            pltpu.SemaphoreType.DMA((CHANS - 1,)),
            pltpu.SemaphoreType.DMA((CHANS - 1,)),
            pltpu.SemaphoreType.DMA,
            pltpu.SemaphoreType.DMA,
        ],
        compiler_params=pltpu.CompilerParams(
            collective_id=0, has_side_effects=True, vmem_limit_bytes=40 * MIB
        ),
    )(ready, weights, x_forward, x_inverse)


def inverse_kernel(modes_ref, field_ref, table_ref, bias_ref, out_ref, lhs_ref):
    plane, chunk = pl.program_id(0), pl.program_id(1)
    rows_y = field_ref.shape[1]

    @pl.when(chunk == 0)
    def _():
        turned = []
        for ky_half in range(2):
            piece = jnp.concatenate(
                [
                    modes_ref[
                        pl.ds(plane * 8 + ky_half * 4 + part, SLABS, stride=BLOCK), :
                    ]
                    for part in range(4)
                ],
                axis=0,
            )
            turned.append(piece.T)
        for group in range(CL // 16):
            kept = [
                turned[k // 4][k % 4 * CL + group * 16 : k % 4 * CL + group * 16 + 16]
                for k in range(MY)
            ]
            spun = [None] + [rotate_parts(kept[k], -1.0) for k in range(1, MY)]

            def put(y, value):
                high = value.astype(jnp.bfloat16)
                low = (value - high.astype(jnp.float32)).astype(jnp.bfloat16)
                rows = pl.ds(y * CL + group * 16, 16)
                lhs_ref[rows, :LANES] = high
                lhs_ref[rows, LANES:] = low

            half = GY // 2
            even, odd = total(kept[0::2]), total(kept[1::2])
            put(0, even + odd)
            put(half, even - odd)
            even = (kept[0] + kept[4]) - (kept[2] + kept[6])
            odd = (spun[1] + spun[5]) - (spun[3] + spun[7])
            put(half // 2, even + odd)
            put(half // 2 + half, even - odd)
            for y in range(1, half // 2):
                cos_even = total([kept[0]] + [cos_y(k, y) * kept[k] for k in (2, 4, 6)])
                cos_odd = total([cos_y(k, y) * kept[k] for k in (1, 3, 5, 7)])
                sin_even = total([sin_y(k, y) * spun[k] for k in (2, 4, 6)])
                sin_odd = total([sin_y(k, y) * spun[k] for k in (1, 3, 5, 7)])
                cos_sum, cos_dif = cos_even + cos_odd, cos_even - cos_odd
                sin_sum, sin_dif = sin_even + sin_odd, sin_odd - sin_even
                put(y, cos_sum + sin_sum)
                put(GY - y, cos_sum - sin_sum)
                put(half - y, cos_dif + sin_dif)
                put(half + y, cos_dif - sin_dif)

    bias = bias_ref[...]
    step_y = 4

    def step(i, carry):
        start = pl.multiple_of(chunk * (rows_y * CL) + i * (step_y * CL), step_y * CL)
        high = lhs_ref[pl.ds(start, step_y * CL), :LANES]
        low = lhs_ref[pl.ds(start, step_y * CL), LANES:]
        branch = dot(jnp.concatenate([high, low, high], axis=1), table_ref[...])
        h = branch.reshape(step_y, CL, ZT) + bias[None]
        square = h * h
        poly = GELU_H[6]
        for coefficient in GELU_H[5::-1]:
            poly = poly * square + coefficient
        value = h + h * jnp.tanh(h * poly)
        at = pl.ds(i * step_y, step_y)
        out_ref[0, at] = field_ref[0, at].astype(jnp.float32) + value
        return carry

    lax.fori_loop(0, rows_y // step_y, step, 0)


def inverse(modes, field, table, bias):
    rows_y = 16
    return pl.pallas_call(
        inverse_kernel,
        grid=(XL, GY // rows_y),
        in_specs=[
            pl.BlockSpec((SLABS * BLOCK, LANES), lambda x, y: (0, 0)),
            pl.BlockSpec((1, rows_y, CL, ZT), lambda x, y: (x, y, 0, 0)),
            pl.BlockSpec((3 * LANES, ZT), lambda x, y: (0, 0)),
            pl.BlockSpec((CL, 1), lambda x, y: (0, 0)),
        ],
        out_specs=pl.BlockSpec((1, rows_y, CL, ZT), lambda x, y: (x, y, 0, 0)),
        out_shape=jax.ShapeDtypeStruct((XL, GY, CL, ZT), jnp.float32),
        scratch_shapes=[pltpu.VMEM((GY * CL, 2 * LANES), jnp.bfloat16)],
        compiler_params=pltpu.CompilerParams(vmem_limit_bytes=32 * MIB),
    )(modes, field, table, bias)


def shards(field, spectral_weights, bias):
    weights = spectral_weights.reshape(2, QL * MX, MY * CL, LANES)
    ready = forward(field, jnp.asarray(forward_zt_table()))
    back = exchange(
        ready, weights, jnp.asarray(forward_x_table()), jnp.asarray(inverse_x_table())
    )
    half_bias = (0.5 * bias).reshape(CL, 1)
    return inverse(back, field, jnp.asarray(inverse_zt_table()), half_bias)


def solution(mesh):
    return jax.shard_map(
        shards,
        mesh=mesh,
        in_specs=(
            P("slab", None, "chan", None),
            P(None, "slab", None, None, "chan", None),
            P("chan"),
        ),
        out_specs=P("slab", None, "chan", None),
        check_vma=False,
    )
```

profile of v0, /device:TPU:1, one launch (start us, length us, event | category | flops | bytes accessed | tf_op | source)
XLA Modules:
  0.0 50.6 jit_solution(6056239328017181700)
XLA Ops:
  0.0 0.0 copy-start.6
  0.0 0.7 %multiply_bitcast_fusion = f32[32,1]{0,1:T(1,128)S(1)} fusion(f32[32]{0:T(128)} %param.9), kind=kLoop, calls=%fused_computation | loop fusion | flops 32 | bytes 256 | tf_op jit(solution)/shard_map/reshape | solution.py:507
  0.7 0.1 copy.8.bias_ref
  0.8 0.0 copy-start
  0.8 2.2 %copy-done = bf16[2,64,32,512]{3,2,1,0:T(8,128)(2,1)S(1)} copy-done((bf16[2,64,32,512]{3,2,1,0:T(8,128)(2,1)S(1)}, bf16[2,64,32,512]{3,2,1,0:T(8,128)(2,1)}, u32[]{:S(2)}) %copy-start) | copy-done | bytes 4194328
  3.0 0.0 copy-start.4
  3.0 0.9 %copy-done.4 = bf16[512,256]{1,0:T(8,128)(2,1)S(1)} copy-done((bf16[512,256]{1,0:T(8,128)(2,1)S(1)}, bf16[512,256]{1,0:T(8,128)(2,1)}, u32[]{:S(2)}) %copy-start.4) | copy-done | bytes 262168
  3.9 0.0 copy-start.5
  3.9 0.0 copy-start.1
  3.9 0.0 copy-start.3
  3.9 3.3 %shard_map.73.ready_ref = f32[512,128]{1,0:T(8,128)S(1)} custom-call(bf16[2,64,32,512]{3,2,1,0:T(8,128)(2,1)S(1)} %copy-done, bf16[512,256]{1,0:T(8,128)(2,1)S(1)} %copy-done.4), custom_call_target="tpu_custom_call" | custom-call | tf_op jit(solution)/shard_map/pallas_call | solution.py:165
  7.2 0.0 copy-done.6
  7.2 0.0 copy-done.5
  7.2 0.0 copy-start.2
  7.2 2.2 %copy-done.2 = f32[2,2,8,8,32,128]{5,4,3,2,1,0:T(8,128)S(1)} copy-done((f32[2,2,8,8,32,128]{5,4,3,2,1,0:T(8,128)S(1)}, f32[2,2,8,8,32,128]{5,4,3,2,1,0:T(8,128)}, u32[]{:S(2)}) %copy-start.2) | copy-done | bytes 4194328
  9.4 26.7 %shard_map.74.modes_ref = f32[512,128]{1,0:T(8,128)S(1)} custom-call(f32[512,128]{1,0:T(8,128)S(1)} %shard_map.73.ready_ref, f32[2,16,256,128]{3,2,1,0:T(8,128)S(1)} %bitcast.3, f32[16,128]{1,0:T(8,128)S(1)} %copy-done.6, f32[128,16]{1,0:T(8,128)S(1)} %copy-done.5), custom_call_target="tpu_custom_call" | custom-call | tf_op jit(solution)/shard_map/pallas_call | solution.py:380
  36.2 0.0 copy-done.1
  36.2 0.0 copy-done.3
  36.2 14.4 %shard_map.75 = f32[2,64,32,512]{3,2,1,0:T(8,128)} custom-call(f32[512,128]{1,0:T(8,128)S(1)} %shard_map.74.modes_ref, bf16[2,64,32,512]{3,2,1,0:T(8,128)(2,1)S(1)} %copy-done.1, bf16[384,512]{1,0:T(8,128)(2,1)S(1)} %copy-done.3, f32[32,1]{1,0:T(8,128)S(1)} %copy.8.bias_ref), custom_call_target="tpu_custom_call" | custom-call | tf_op jit(solution)/shard_map/pallas_call | solution.py:485
Async XLA Ops:
  0.0 7.2 %copy-start.6 = (f32[16,128]{1,0:T(8,128)S(1)}, f32[16,128]{1,0:T(8,128)}, u32[]{:S(2)}) copy-start(f32[16,128]{1,0:T(8,128)} %constant.11.clone.x_forward_ref) | copy-start | bytes 24580
  0.8 2.2 %copy-start = (bf16[2,64,32,512]{3,2,1,0:T(8,128)(2,1)S(1)}, bf16[2,64,32,512]{3,2,1,0:T(8,128)(2,1)}, u32[]{:S(2)}) copy-start(bf16[2,64,32,512]{3,2,1,0:T(8,128)(2,1)} %field_ref.3) | copy-start | bytes 12582916
  3.0 0.9 %copy-start.4 = (bf16[512,256]{1,0:T(8,128)(2,1)S(1)}, bf16[512,256]{1,0:T(8,128)(2,1)}, u32[]{:S(2)}) copy-start(bf16[512,256]{1,0:T(8,128)(2,1)} %constant.10.clone.table_ref) | copy-start | bytes 786436
  3.9 3.3 %copy-start.5 = (f32[128,16]{1,0:T(8,128)S(1)}, f32[128,16]{1,0:T(8,128)}, u32[]{:S(2)}) copy-start(f32[128,16]{1,0:T(8,128)} %constant.12.clone.x_inverse_ref) | copy-start | bytes 24580
  3.9 32.3 %copy-start.1 = (bf16[2,64,32,512]{3,2,1,0:T(8,128)(2,1)S(1)}, bf16[2,64,32,512]{3,2,1,0:T(8,128)(2,1)}, u32[]{:S(2)}) copy-start(bf16[2,64,32,512]{3,2,1,0:T(8,128)(2,1)} %field_ref.3) | copy-start | bytes 12582916
  3.9 32.3 %copy-start.3 = (bf16[384,512]{1,0:T(8,128)(2,1)S(1)}, bf16[384,512]{1,0:T(8,128)(2,1)}, u32[]{:S(2)}) copy-start(bf16[384,512]{1,0:T(8,128)(2,1)} %constant.13.clone.table_ref) | copy-start | bytes 1179652
  7.2 2.2 %copy-start.2 = (f32[2,2,8,8,32,128]{5,4,3,2,1,0:T(8,128)S(1)}, f32[2,2,8,8,32,128]{5,4,3,2,1,0:T(8,128)}, u32[]{:S(2)}) copy-start(f32[2,2,8,8,32,128]{5,4,3,2,1,0:T(8,128)} %param.8) | copy-start | bytes 12582916
where the time goes:
time: 50.8 us; the launch traced here: 50.6 us
  Pallas kernels  44.4 us (87%)
  local copies, waits for them, and re-layouts  5.42 us (11%)
  other arithmetic  0.67 us (1%)
    pallas_call x1, Pallas kernels, exchange(): pl.pallas_call(exchange_kernel, in_specs=[vmem, pl.BlockSpec(memory_space...  26.7 us
    pallas_call x1, Pallas kernels, inverse(): pl.pallas_call(inverse_kernel, grid=(XL, GY // rows_y), in_specs=[pl.Bloc...  14.4 us
    unnamed x14, local copies, waits for them, and re-layouts  5.33 us
    pallas_call x1, Pallas kernels, forward(): pl.pallas_call(forward_kernel, grid=(XL, GY // rows_y), in_specs=[pl.Bloc...  3.3 us

commit v1 on v0

--- a/solution.py
+++ b/solution.py
@@ -20,18 +20,11 @@
 LANES = 128
 BLOCK = 16
 MESH = pl.DeviceIdType.MESH
-MIB = 1 << 20
-
-GELU_Q = (
-    7.97884216e-01,
-    3.63342835e-02,
-    -3.31299940e-05,
-    -5.52401584e-05,
-    3.96910946e-06,
-    -1.33446409e-07,
-    1.80561642e-09,
-)
-GELU_H = tuple(c * 2.0 * 4.0**k for k, c in enumerate(GELU_Q))
+VMEM_LIMIT = 62 << 20
+CHUNKS = 2
+
+DC_SCALE = float(GX * GY * GZ * GT)
+ROOT_HALF = math.sqrt(0.5)
 
 
 def split_bf16(table):
@@ -56,7 +49,7 @@
 
 def inverse_zt_table():
     angles, modes = zt_angles()
-    weight = np.where(modes % MT == 0, 1.0, 2.0) / (GX * GY * GZ * GT) / 2.0
+    weight = np.where(modes % MT == 0, 1.0, 2.0) * (ROOT_HALF / (GX * GY * GZ * GT))
     table = np.concatenate([weight * np.cos(angles), -weight * np.sin(angles)], axis=1).T
     high, low = split_bf16(table)
     return np.concatenate([high, high, low], axis=0)
@@ -106,85 +99,64 @@
     return jnp.where(lane < LANES // 2, sign, -sign) * swapped
 
 
-def forward_kernel(field_ref, table_ref, out_ref, modes_ref, kept_ref):
-    plane, chunk = pl.program_id(0), pl.program_id(1)
-    chunks = pl.num_programs(1)
-    rows_y = field_ref.shape[1]
-    both = dot(field_ref[...].reshape(rows_y * CL, ZT), table_ref[...])
-    modes_ref[pl.ds(chunk * rows_y, rows_y)] = (both[:, :LANES] + both[:, LANES:]).reshape(
-        rows_y, CL, LANES
-    )
-
-    @pl.when(chunk == chunks - 1)
-    def _():
-        half = GY // 2
-        for group in range(CL // 8):
-            rows = pl.ds(group * 8, 8)
-
-            def load(y):
-                return modes_ref[y, rows, :]
-
-            first, middle = load(0), load(half)
-            even, odd = first + middle, first - middle
-            cosines = [even if k % 2 == 0 else odd for k in range(MY)]
-            first, middle = load(half // 2), load(half // 2 + half)
-            even, odd = first + middle, first - middle
-            sines = [None] * MY
+def forward_y(modes_ref, kept_ref, out_ref, plane):
+    half = GY // 2
+    for group in range(CL // 8):
+        rows = pl.ds(group * 8, 8)
+
+        def load(y):
+            return modes_ref[y, rows, :]
+
+        first, middle = load(0), load(half)
+        even, odd = first + middle, first - middle
+        cosines = [even if k % 2 == 0 else odd for k in range(MY)]
+        first, middle = load(half // 2), load(half // 2 + half)
+        even, odd = first + middle, first - middle
+        sines = [None] * MY
+        for k in range(MY):
+            if k % 2 == 0:
+                cosines[k] = cosines[k] + (even if k % 4 == 0 else -even)
+            else:
+                sines[k] = odd if k % 4 == 1 else -odd
+        for y in range(1, half // 2):
+            a, b, c, d = load(y), load(GY - y), load(half - y), load(half + y)
+            sum1, dif1, sum2, dif2 = a + b, a - b, c + d, c - d
+            for_even, for_odd = sum1 + sum2, sum1 - sum2
+            sin_odd, sin_even = dif1 + dif2, dif1 - dif2
             for k in range(MY):
-                if k % 2 == 0:
-                    cosines[k] = cosines[k] + (even if k % 4 == 0 else -even)
-                else:
-                    sines[k] = odd if k % 4 == 1 else -odd
-            for y in range(1, half // 2):
-                a, b, c, d = load(y), load(GY - y), load(half - y), load(half + y)
-                sum1, dif1, sum2, dif2 = a + b, a - b, c + d, c - d
-                for_even, for_odd = sum1 + sum2, sum1 - sum2
-                sin_odd, sin_even = dif1 + dif2, dif1 - dif2
-                for k in range(MY):
-                    cosines[k] = cosines[k] + cos_y(k, y) * (for_even if k % 2 == 0 else for_odd)
-                    if k > 0:
-                        term = sin_y(k, y) * (sin_even if k % 2 == 0 else sin_odd)
-                        sines[k] = term if sines[k] is None else sines[k] + term
-            for k in range(MY):
-                value = cosines[k]
+                cosines[k] = cosines[k] + cos_y(k, y) * (for_even if k % 2 == 0 else for_odd)
                 if k > 0:
-                    value = value + rotate_parts(sines[k], 1.0)
-                kept_ref[pl.ds(k * CL + group * 8, 8), :] = value
-        for ky_half in range(2):
-            turned = kept_ref[pl.ds(ky_half * LANES, LANES), :].T
-            for part in range(4):
-                for owners in range(SLABS // 8):
-                    start = owners * 8 * BLOCK + plane * 8 + ky_half * 4 + part
-                    out_ref[pl.ds(start, 8, stride=BLOCK), :] = turned[
-                        part * SLABS + owners * 8 : part * SLABS + owners * 8 + 8
-                    ]
-
-
-def forward(field, table):
-    rows_y = 16
-    return pl.pallas_call(
-        forward_kernel,
-        grid=(XL, GY // rows_y),
-        in_specs=[
-            pl.BlockSpec((1, rows_y, CL, ZT), lambda x, y: (x, y, 0, 0)),
-            pl.BlockSpec((ZT, 2 * LANES), lambda x, y: (0, 0)),
-        ],
-        out_specs=pl.BlockSpec((SLABS * BLOCK, LANES), lambda x, y: (0, 0)),
-        out_shape=jax.ShapeDtypeStruct((SLABS * BLOCK, LANES), jnp.float32),
-        scratch_shapes=[
-            pltpu.VMEM((GY, CL, LANES), jnp.float32),
-            pltpu.VMEM((MY * CL, LANES), jnp.float32),
-        ],
-        compiler_params=pltpu.CompilerParams(vmem_limit_bytes=32 * MIB),
-    )(field, table)
+                    term = sin_y(k, y) * (sin_even if k % 2 == 0 else sin_odd)
+                    sines[k] = term if sines[k] is None else sines[k] + term
+        for k in range(MY):
+            value = cosines[k]
+            if k > 0:
+                value = value + rotate_parts(sines[k], 1.0)
+            kept_ref[pl.ds(k * CL + group * 8, 8), :] = value
+    for ky_half in range(2):
+        turned = kept_ref[pl.ds(ky_half * LANES, LANES), :].T
+        for part in range(4):
+            for owners in range(SLABS // 8):
+                start = owners * 8 * BLOCK + plane * 8 + ky_half * 4 + part
+                out_ref[pl.ds(start, 8, stride=BLOCK), :] = turned[
+                    part * SLABS + owners * 8 : part * SLABS + owners * 8 + 8
+                ]
 
 
 def exchange_kernel(
-    ready_ref,
+    field_ref,
     weights_ref,
+    zt_hbm,
+    x_forward_hbm,
+    x_inverse_hbm,
+    out_ref,
+    zt_ref,
     x_forward_ref,
     x_inverse_ref,
-    out_ref,
+    field_in,
+    modes_ref,
+    kept_ref,
+    ready_ref,
     arrived,
     staged,
     high_ref,
@@ -194,6 +166,8 @@
     parcels,
     parcels_in,
     outgoing,
+    table_sem,
+    field_sem,
     weight_sem,
     local_sem,
     send_sem,
@@ -209,6 +183,26 @@
     def weight_copy(part):
         return pltpu.make_async_copy(weights_ref.at[part], staged.at[part], weight_sem.at[part])
 
+    chunk = GY // CHUNKS
+
+    def field_copy(plane, piece):
+        rows = pl.ds(piece * chunk, chunk)
+        return pltpu.make_async_copy(
+            field_ref.at[plane, rows], field_in.at[plane, rows], field_sem.at[plane, piece]
+        )
+
+    table_copies = [
+        pltpu.make_async_copy(source, target, table_sem.at[i])
+        for i, (source, target) in enumerate(
+            [(zt_hbm, zt_ref), (x_forward_hbm, x_forward_ref), (x_inverse_hbm, x_inverse_ref)]
+        )
+    ]
+    table_copies[0].start()
+    for plane in range(XL):
+        for piece in range(CHUNKS):
+            field_copy(plane, piece).start()
+    for copy in table_copies[1:]:
+        copy.start()
     for part in range(2):
         weight_copy(part).start()
 
@@ -228,6 +222,17 @@
 
     lax.fori_loop(1, SLABS, greet_slab, 0)
     lax.fori_loop(1, CHANS, greet_chan, 0)
+    table_copies[0].wait()
+
+    for plane in range(XL):
+        for piece in range(CHUNKS):
+            field_copy(plane, piece).wait()
+            rows = pl.ds(piece * chunk, chunk)
+            both = dot(field_in[plane, rows].reshape(chunk * CL, ZT), zt_ref[...])
+            both = both[:, :LANES] + both[:, LANES:]
+            modes_ref[rows] = both.reshape(chunk, CL, LANES)
+        forward_y(modes_ref, kept_ref, ready_ref, plane)
+
     pl.semaphore_wait(barrier, SLABS + CHANS - 2)
 
     def block_of(owner):
@@ -272,6 +277,8 @@
 
         lax.fori_loop(0, QL * MX, split_weights, 0)
 
+    for copy in table_copies[1:]:
+        copy.wait()
     own.wait()
     rows_sent = (SLABS - 1) * BLOCK
     wait_bytes(arrived, rows_sent, recv_sem)
@@ -374,15 +381,23 @@
     wait_bytes(outgoing, rows_sent, back_send)
 
 
-def exchange(ready, weights, x_forward, x_inverse):
+def exchange(field, weights, zt_table, x_forward, x_inverse):
     vmem = pl.BlockSpec(memory_space=pltpu.VMEM)
+    hbm = pl.BlockSpec(memory_space=pl.ANY)
     rows = SLABS * BLOCK
     return pl.pallas_call(
         exchange_kernel,
-        in_specs=[vmem, pl.BlockSpec(memory_space=pl.ANY), vmem, vmem],
+        in_specs=[hbm] * 5,
         out_specs=vmem,
         out_shape=jax.ShapeDtypeStruct((rows, LANES), jnp.float32),
         scratch_shapes=[
+            pltpu.VMEM((ZT, 2 * LANES), jnp.bfloat16),
+            pltpu.VMEM((2 * MX, 2 * GX), jnp.float32),
+            pltpu.VMEM((2 * GX, 2 * MX), jnp.float32),
+            pltpu.VMEM((XL, GY, CL, ZT), jnp.bfloat16),
+            pltpu.VMEM((GY, CL, LANES), jnp.float32),
+            pltpu.VMEM((MY * CL, LANES), jnp.float32),
+            pltpu.VMEM((rows, LANES), jnp.float32),
             pltpu.VMEM((rows, LANES), jnp.float32),
             pltpu.VMEM((2, QL * MX, 256, LANES), jnp.float32),
             pltpu.VMEM((QL * MX, 256, 256), jnp.bfloat16),
@@ -392,6 +407,8 @@
             pltpu.VMEM((CHANS, 64, LANES), jnp.float32),
             pltpu.VMEM((CHANS - 1, 64, LANES), jnp.float32),
             pltpu.VMEM((rows, LANES), jnp.float32),
+            pltpu.SemaphoreType.DMA((3,)),
+            pltpu.SemaphoreType.DMA((XL, CHUNKS)),
             pltpu.SemaphoreType.DMA((2,)),
             pltpu.SemaphoreType.DMA,
             pltpu.SemaphoreType.DMA,
@@ -402,17 +419,19 @@
             pltpu.SemaphoreType.DMA,
         ],
         compiler_params=pltpu.CompilerParams(
-            collective_id=0, has_side_effects=True, vmem_limit_bytes=40 * MIB
+            collective_id=0, has_side_effects=True, vmem_limit_bytes=VMEM_LIMIT
         ),
-    )(ready, weights, x_forward, x_inverse)
-
-
-def inverse_kernel(modes_ref, field_ref, table_ref, bias_ref, out_ref, lhs_ref):
+    )(field, weights, zt_table, x_forward, x_inverse)
+
+
+def inverse_kernel(modes_ref, field_ref, table_ref, bias_ref, out_ref, lhs_ref, shift_ref):
     plane, chunk = pl.program_id(0), pl.program_id(1)
     rows_y = field_ref.shape[1]
 
     @pl.when(chunk == 0)
     def _():
+        shift_ref[...] = jnp.zeros_like(shift_ref)
+        shift_ref[0:1, :CL] = bias_ref[...] * DC_SCALE
         turned = []
         for ky_half in range(2):
             piece = jnp.concatenate(
@@ -424,6 +443,8 @@
                 ],
                 axis=0,
             )
+            if ky_half == 0:
+                piece = jnp.concatenate([piece[:8] + shift_ref[...], piece[8:]], axis=0)
             turned.append(piece.T)
         for group in range(CL // 16):
             kept = [
@@ -459,25 +480,11 @@
                 put(half - y, cos_dif + sin_dif)
                 put(half + y, cos_dif - sin_dif)
 
-    bias = bias_ref[...]
-    step_y = 4
-
-    def step(i, carry):
-        start = pl.multiple_of(chunk * (rows_y * CL) + i * (step_y * CL), step_y * CL)
-        high = lhs_ref[pl.ds(start, step_y * CL), :LANES]
-        low = lhs_ref[pl.ds(start, step_y * CL), LANES:]
-        branch = dot(jnp.concatenate([high, low, high], axis=1), table_ref[...])
-        h = branch.reshape(step_y, CL, ZT) + bias[None]
-        square = h * h
-        poly = GELU_H[6]
-        for coefficient in GELU_H[5::-1]:
-            poly = poly * square + coefficient
-        value = h + h * jnp.tanh(h * poly)
-        at = pl.ds(i * step_y, step_y)
-        out_ref[0, at] = field_ref[0, at].astype(jnp.float32) + value
-        return carry
-
-    lax.fori_loop(0, rows_y // step_y, step, 0)
+    rows = pl.ds(pl.multiple_of(chunk * (rows_y * CL), rows_y * CL), rows_y * CL)
+    high, low = lhs_ref[rows, :LANES], lhs_ref[rows, LANES:]
+    scaled = dot(jnp.concatenate([high, low, high], axis=1), table_ref[...])
+    value = (ROOT_HALF * scaled) * (1.0 + lax.erf(scaled))
+    out_ref[0] = field_ref[0].astype(jnp.float32) + value.reshape(rows_y, CL, ZT)
 
 
 def inverse(modes, field, table, bias):
@@ -489,23 +496,28 @@
             pl.BlockSpec((SLABS * BLOCK, LANES), lambda x, y: (0, 0)),
             pl.BlockSpec((1, rows_y, CL, ZT), lambda x, y: (x, y, 0, 0)),
             pl.BlockSpec((3 * LANES, ZT), lambda x, y: (0, 0)),
-            pl.BlockSpec((CL, 1), lambda x, y: (0, 0)),
+            pl.BlockSpec((1, CL), lambda x, y: (0, 0)),
         ],
         out_specs=pl.BlockSpec((1, rows_y, CL, ZT), lambda x, y: (x, y, 0, 0)),
         out_shape=jax.ShapeDtypeStruct((XL, GY, CL, ZT), jnp.float32),
-        scratch_shapes=[pltpu.VMEM((GY * CL, 2 * LANES), jnp.bfloat16)],
-        compiler_params=pltpu.CompilerParams(vmem_limit_bytes=32 * MIB),
+        scratch_shapes=[
+            pltpu.VMEM((GY * CL, 2 * LANES), jnp.bfloat16),
+            pltpu.VMEM((8, LANES), jnp.float32),
+        ],
+        compiler_params=pltpu.CompilerParams(vmem_limit_bytes=VMEM_LIMIT),
     )(modes, field, table, bias)
 
 
 def shards(field, spectral_weights, bias):
     weights = spectral_weights.reshape(2, QL * MX, MY * CL, LANES)
-    ready = forward(field, jnp.asarray(forward_zt_table()))
     back = exchange(
-        ready, weights, jnp.asarray(forward_x_table()), jnp.asarray(inverse_x_table())
+        field,
+        weights,
+        jnp.asarray(forward_zt_table()),
+        jnp.asarray(forward_x_table()),
+        jnp.asarray(inverse_x_table()),
     )
-    half_bias = (0.5 * bias).reshape(CL, 1)
-    return inverse(back, field, jnp.asarray(inverse_zt_table()), half_bias)
+    return inverse(back, field, jnp.asarray(inverse_zt_table()), bias.reshape(1, CL))
 
 
 def solution(mesh):

time: 50.8 us -> 38.3 us (0.75)
  Pallas kernels: 44.4 us -> 38 us
  local copies, waits for them, and re-layouts: 5.42 us -> 0 us
  other arithmetic: 0.67 us -> 0 us
    unnamed x14 -> x0, local copies, waits for them, and re-layouts: 5.33 us -> none
    pallas_call x1, Pallas kernels: 14.4 us -> 10.2 us  [inverse(): pl.pallas_call(inverse_kernel, grid=(XL, GY // rows_y), in_specs=[pl.Bloc...]
    pallas_call x2 -> x1, Pallas kernels: 30 us -> 27.8 us  [exchange(): pl.pallas_call(exchange_kernel, in_specs=[hbm] * 5, out_specs=vmem, out_s...]
    reshape x1 -> x0, other arithmetic: 0.67 us -> none  [shards(): half_bias = (0.5 * bias).reshape(CL, 1)]
where the time goes in v1:
time: 38.3 us; the launch traced here: 38 us
  Pallas kernels  38 us (99%)
    pallas_call x1, Pallas kernels, exchange(): pl.pallas_call(exchange_kernel, in_specs=[hbm] * 5, out_specs=vmem, out_s...  27.8 us
    pallas_call x1, Pallas kernels, inverse(): pl.pallas_call(inverse_kernel, grid=(XL, GY // rows_y), in_specs=[pl.Bloc...  10.2 us

profile of v1, /device:TPU:1, one launch (start us, length us, event | category | flops | bytes accessed | tf_op | source)
XLA Modules:
  0.0 38.0 jit_solution(5536560383497742964)
XLA Ops:
  0.0 27.8 %shard_map.73.modes_ref = f32[512,128]{1,0:T(8,128)} custom-call(bf16[2,64,32,512]{3,2,1,0:T(8,128)(2,1)} %field_ref.3, f32[2,16,256,128]{3,2,1,0:T(8,128)} %bitcast.2, bf16[512,256]{1,0:T(8,128)(2,1)} %constant.8.clone.zt_hbm, f32[16,128]{1,0:T(8,128)} %constant.9.clone.x_forward_hbm, f32[128,16]{1,0:T(8,128)} %constant.10.clone.x_inverse_hbm), custom_call_target="tpu_custom_call" | custom-call | tf_op jit(solution)/shard_map/pallas_call | solution.py:388
  27.8 10.2 %shard_map.74 = f32[2,64,32,512]{3,2,1,0:T(8,128)} custom-call(f32[512,128]{1,0:T(8,128)} %shard_map.73.modes_ref, bf16[2,64,32,512]{3,2,1,0:T(8,128)(2,1)} %field_ref.3, bf16[384,512]{1,0:T(8,128)(2,1)} %constant.11.clone.table_ref, f32[1,32]{1,0:T(1,128)} %bitcast.3), custom_call_target="tpu_custom_call" | custom-call | tf_op jit(solution)/shard_map/pallas_call | solution.py:492

commit v2 on v1

--- a/solution.py
+++ b/solution.py
@@ -20,7 +20,7 @@
 LANES = 128
 BLOCK = 16
 MESH = pl.DeviceIdType.MESH
-VMEM_LIMIT = 62 << 20
+VMEM_LIMIT = 40 << 20
 CHUNKS = 2
 
 DC_SCALE = float(GX * GY * GZ * GT)
@@ -48,11 +48,25 @@
 
 
 def inverse_zt_table():
-    angles, modes = zt_angles()
-    weight = np.where(modes % MT == 0, 1.0, 2.0) * (ROOT_HALF / (GX * GY * GZ * GT))
-    table = np.concatenate([weight * np.cos(angles), -weight * np.sin(angles)], axis=1).T
-    high, low = split_bf16(table)
-    return np.concatenate([high, high, low], axis=0)
+    cells = np.arange(ZT // 2)[None, :]
+    row = np.arange(KQ // 2)[:, None]
+    tables = []
+    for odd in range(2):
+        kz = 2 * (row // 4 % 4) + odd
+        kt = 2 * (row % 4) + row // 16
+        counted = kz * (cells // GT) % GZ * GT + kt * (cells % GT) % GT * GZ
+        angles = 2.0 * math.pi * counted / (GZ * GT)
+        weight = np.where(kt == 0, 1.0, 2.0) * (ROOT_HALF / (GX * GY * GZ * GT))
+        tables.append(np.concatenate([weight * np.cos(angles), -weight * np.sin(angles)], axis=0))
+    (even, even_low), (odd, odd_low) = map(split_bf16, tables)
+    zero = np.zeros_like(even)
+    return np.concatenate(
+        [
+            np.concatenate([even, even, even_low, zero], axis=0),
+            np.concatenate([zero, odd_low, odd, odd], axis=0),
+        ],
+        axis=1,
+    )
 
 
 def forward_x_table():
@@ -93,10 +107,17 @@
     return terms[0]
 
 
-def rotate_parts(values, sign):
-    lane = lax.broadcasted_iota(jnp.int32, values.shape, values.ndim - 1)
-    swapped = pltpu.roll(values, LANES // 2, values.ndim - 1)
-    return jnp.where(lane < LANES // 2, sign, -sign) * swapped
+def rotate_forward(values):
+    lane = lax.broadcasted_iota(jnp.int32, values.shape, 1)
+    swapped = pltpu.roll(values, LANES // 2, 1)
+    return jnp.where(lane < LANES // 2, swapped, -swapped)
+
+
+def rotate_inverse(values):
+    lane = lax.broadcasted_iota(jnp.int32, values.shape, 1)
+    ahead = pltpu.roll(values, LANES - 32, 1)
+    behind = pltpu.roll(values, 32, 1)
+    return jnp.where(lane % 64 < 32, -ahead, behind)
 
 
 def forward_y(modes_ref, kept_ref, out_ref, plane):
@@ -131,7 +152,7 @@
         for k in range(MY):
             value = cosines[k]
             if k > 0:
-                value = value + rotate_parts(sines[k], 1.0)
+                value = value + rotate_forward(sines[k])
             kept_ref[pl.ds(k * CL + group * 8, 8), :] = value
     for ky_half in range(2):
         turned = kept_ref[pl.ds(ky_half * LANES, LANES), :].T
@@ -149,11 +170,16 @@
     zt_hbm,
     x_forward_hbm,
     x_inverse_hbm,
+    zt_back_hbm,
+    bias_hbm,
     out_ref,
+    field_in,
+    zt_back_ref,
     zt_ref,
     x_forward_ref,
     x_inverse_ref,
-    field_in,
+    bias_ref,
+    shift_ref,
     modes_ref,
     kept_ref,
     ready_ref,
@@ -194,17 +220,24 @@
     table_copies = [
         pltpu.make_async_copy(source, target, table_sem.at[i])
         for i, (source, target) in enumerate(
-            [(zt_hbm, zt_ref), (x_forward_hbm, x_forward_ref), (x_inverse_hbm, x_inverse_ref)]
+            [
+                (zt_hbm, zt_ref),
+                (x_forward_hbm, x_forward_ref),
+                (x_inverse_hbm, x_inverse_ref),
+                (bias_hbm, bias_ref),
+                (zt_back_hbm, zt_back_ref),
+            ]
         )
     ]
     table_copies[0].start()
     for plane in range(XL):
         for piece in range(CHUNKS):
             field_copy(plane, piece).start()
-    for copy in table_copies[1:]:
+    for copy in table_copies[1:4]:
         copy.start()
     for part in range(2):
         weight_copy(part).start()
+    table_copies[4].start()
 
     barrier = pltpu.get_barrier_semaphore()
 
@@ -238,12 +271,12 @@
     def block_of(owner):
         return pl.ds(pl.multiple_of(owner * BLOCK, BLOCK), BLOCK)
 
-    def send_all(source, target, send, recv):
+    def send_all(source, target, place, send, recv):
         def step(i, carry):
             other = lax.rem(slab + i, SLABS)
             pltpu.make_async_remote_copy(
                 src_ref=source.at[block_of(other)],
-                dst_ref=target.at[block_of(slab)],
+                dst_ref=target.at[block_of(place)],
                 send_sem=send,
                 recv_sem=recv,
                 device_id=(other, chan),
@@ -253,7 +286,7 @@
 
         lax.fori_loop(1, SLABS, step, 0)
         own = pltpu.make_async_copy(
-            source.at[block_of(slab)], target.at[block_of(slab)], local_sem
+            source.at[block_of(slab)], target.at[block_of(place)], local_sem
         )
         own.start()
         return own
@@ -262,7 +295,7 @@
         piece = ref.at[pl.ds(0, rows)]
         pltpu.make_async_copy(piece, piece, sem).wait()
 
-    own = send_all(ready_ref, arrived, send_sem, recv_sem)
+    own = send_all(ready_ref, arrived, slab, send_sem, recv_sem)
 
     for part in range(2):
         weight_copy(part).wait()
@@ -362,6 +395,11 @@
         chan_copies[i - 1].wait_recv()
         mixed = mixed + parcels_in[i - 1]
 
+    shift_ref[...] = jnp.zeros_like(shift_ref)
+    shift_ref[0:1, :CL] = bias_ref[...] * DC_SCALE
+    shift = jnp.where(slab == 0, shift_ref[...], 0.0)
+    mixed = jnp.concatenate([mixed[:8] + shift, mixed[8:]], axis=0)
+
     side = jnp.concatenate([mixed[16 * i : 16 * i + 16] for i in range(4)], axis=1)
     spatial = dot(x_inverse_ref[...], side, highest)
     for parity in range(QL):
@@ -372,7 +410,8 @@
                     part * GX : (part + 1) * GX, at * LANES : (at + 1) * LANES
                 ]
 
-    own = send_all(outgoing, out_ref, back_send, back_recv)
+    place = slab // 4 % 2 * 16 + slab // 8 * 4 + slab % 4
+    own = send_all(outgoing, out_ref, place, back_send, back_recv)
     own.wait()
     for copy in chan_copies:
         copy.wait_send()
@@ -381,20 +420,23 @@
     wait_bytes(outgoing, rows_sent, back_send)
 
 
-def exchange(field, weights, zt_table, x_forward, x_inverse):
-    vmem = pl.BlockSpec(memory_space=pltpu.VMEM)
-    hbm = pl.BlockSpec(memory_space=pl.ANY)
+def exchange(*operands):
     rows = SLABS * BLOCK
     return pl.pallas_call(
         exchange_kernel,
-        in_specs=[hbm] * 5,
-        out_specs=vmem,
-        out_shape=jax.ShapeDtypeStruct((rows, LANES), jnp.float32),
+        in_specs=[pl.BlockSpec(memory_space=pl.ANY)] * len(operands),
+        out_specs=[pl.BlockSpec(memory_space=pltpu.VMEM)] * 3,
+        out_shape=[
+            pltpu.VMEM((rows, LANES), jnp.float32),
+            pltpu.VMEM((XL, GY, CL, ZT), jnp.bfloat16),
+            pltpu.VMEM((2 * LANES, ZT), jnp.bfloat16),
+        ],
         scratch_shapes=[
             pltpu.VMEM((ZT, 2 * LANES), jnp.bfloat16),
             pltpu.VMEM((2 * MX, 2 * GX), jnp.float32),
             pltpu.VMEM((2 * GX, 2 * MX), jnp.float32),
-            pltpu.VMEM((XL, GY, CL, ZT), jnp.bfloat16),
+            pltpu.VMEM((1, CL), jnp.float32),
+            pltpu.VMEM((8, LANES), jnp.float32),
             pltpu.VMEM((GY, CL, LANES), jnp.float32),
             pltpu.VMEM((MY * CL, LANES), jnp.float32),
             pltpu.VMEM((rows, LANES), jnp.float32),
@@ -407,7 +449,7 @@
             pltpu.VMEM((CHANS, 64, LANES), jnp.float32),
             pltpu.VMEM((CHANS - 1, 64, LANES), jnp.float32),
             pltpu.VMEM((rows, LANES), jnp.float32),
-            pltpu.SemaphoreType.DMA((3,)),
+            pltpu.SemaphoreType.DMA((5,)),
             pltpu.SemaphoreType.DMA((XL, CHUNKS)),
             pltpu.SemaphoreType.DMA((2,)),
             pltpu.SemaphoreType.DMA,
@@ -421,103 +463,119 @@
         compiler_params=pltpu.CompilerParams(
             collective_id=0, has_side_effects=True, vmem_limit_bytes=VMEM_LIMIT
         ),
-    )(field, weights, zt_table, x_forward, x_inverse)
-
-
-def inverse_kernel(modes_ref, field_ref, table_ref, bias_ref, out_ref, lhs_ref, shift_ref):
-    plane, chunk = pl.program_id(0), pl.program_id(1)
-    rows_y = field_ref.shape[1]
-
-    @pl.when(chunk == 0)
-    def _():
-        shift_ref[...] = jnp.zeros_like(shift_ref)
-        shift_ref[0:1, :CL] = bias_ref[...] * DC_SCALE
-        turned = []
-        for ky_half in range(2):
-            piece = jnp.concatenate(
-                [
-                    modes_ref[
-                        pl.ds(plane * 8 + ky_half * 4 + part, SLABS, stride=BLOCK), :
-                    ]
-                    for part in range(4)
-                ],
-                axis=0,
-            )
-            if ky_half == 0:
-                piece = jnp.concatenate([piece[:8] + shift_ref[...], piece[8:]], axis=0)
-            turned.append(piece.T)
-        for group in range(CL // 16):
-            kept = [
-                turned[k // 4][k % 4 * CL + group * 16 : k % 4 * CL + group * 16 + 16]
-                for k in range(MY)
-            ]
-            spun = [None] + [rotate_parts(kept[k], -1.0) for k in range(1, MY)]
-
-            def put(y, value):
-                high = value.astype(jnp.bfloat16)
-                low = (value - high.astype(jnp.float32)).astype(jnp.bfloat16)
-                rows = pl.ds(y * CL + group * 16, 16)
-                lhs_ref[rows, :LANES] = high
-                lhs_ref[rows, LANES:] = low
-
-            half = GY // 2
-            even, odd = total(kept[0::2]), total(kept[1::2])
-            put(0, even + odd)
-            put(half, even - odd)
-            even = (kept[0] + kept[4]) - (kept[2] + kept[6])
-            odd = (spun[1] + spun[5]) - (spun[3] + spun[7])
-            put(half // 2, even + odd)
-            put(half // 2 + half, even - odd)
-            for y in range(1, half // 2):
-                cos_even = total([kept[0]] + [cos_y(k, y) * kept[k] for k in (2, 4, 6)])
-                cos_odd = total([cos_y(k, y) * kept[k] for k in (1, 3, 5, 7)])
-                sin_even = total([sin_y(k, y) * spun[k] for k in (2, 4, 6)])
-                sin_odd = total([sin_y(k, y) * spun[k] for k in (1, 3, 5, 7)])
-                cos_sum, cos_dif = cos_even + cos_odd, cos_even - cos_odd
-                sin_sum, sin_dif = sin_even + sin_odd, sin_odd - sin_even
-                put(y, cos_sum + sin_sum)
-                put(GY - y, cos_sum - sin_sum)
-                put(half - y, cos_dif + sin_dif)
-                put(half + y, cos_dif - sin_dif)
-
-    rows = pl.ds(pl.multiple_of(chunk * (rows_y * CL), rows_y * CL), rows_y * CL)
-    high, low = lhs_ref[rows, :LANES], lhs_ref[rows, LANES:]
-    scaled = dot(jnp.concatenate([high, low, high], axis=1), table_ref[...])
-    value = (ROOT_HALF * scaled) * (1.0 + lax.erf(scaled))
-    out_ref[0] = field_ref[0].astype(jnp.float32) + value.reshape(rows_y, CL, ZT)
-
-
-def inverse(modes, field, table, bias):
-    rows_y = 16
+    )(*[pltpu.with_memory_space_constraint(operand, pltpu.HBM) for operand in operands])
+
+
+def inverse_modes(modes_ref, kept_ref, plane):
+    for ky_half in range(2):
+        piece = jnp.concatenate(
+            [
+                modes_ref[
+                    pl.ds(odd * (16 * BLOCK) + plane * 8 + ky_half * 4 + part, 16, stride=BLOCK), :
+                ]
+                for odd in range(2)
+                for part in range(4)
+            ],
+            axis=0,
+        )
+        turned = piece.T
+        for k in range(4):
+            value = turned[k * CL : k * CL + CL]
+            kept_ref[0, ky_half * 4 + k] = value
+            kept_ref[1, ky_half * 4 + k] = rotate_inverse(value)
+
+
+def inverse_y(kept_ref, y, rows):
+    kept = [kept_ref[0, k, rows, :] for k in range(MY)]
+    spun = [kept_ref[1, k, rows, :] for k in range(MY)]
+    half = GY // 2
+    if y == 0:
+        even, odd = total(kept[0::2]), total(kept[1::2])
+        values = {0: even + odd, half: even - odd}
+        even = (kept[0] + kept[4]) - (kept[2] + kept[6])
+        odd = (spun[1] + spun[5]) - (spun[3] + spun[7])
+        values.update({half // 2: even + odd, half // 2 + half: even - odd})
+        return values
+    cos_even = total([kept[0]] + [cos_y(k, y) * kept[k] for k in (2, 4, 6)])
+    cos_odd = total([cos_y(k, y) * kept[k] for k in (1, 3, 5, 7)])
+    sin_even = total([sin_y(k, y) * spun[k] for k in (2, 4, 6)])
+    sin_odd = total([sin_y(k, y) * spun[k] for k in (1, 3, 5, 7)])
+    cos_sum, cos_dif = cos_even + cos_odd, cos_even - cos_odd
+    sin_sum, sin_dif = sin_even + sin_odd, sin_odd - sin_even
+    return {
+        y: cos_sum + sin_sum,
+        GY - y: cos_sum - sin_sum,
+        half - y: cos_dif + sin_dif,
+        half + y: cos_dif - sin_dif,
+    }
+
+
+def inverse_kernel(modes_ref, field_ref, table_ref, out_hbm, kept_ref, lhs_ref, out_ref, out_sem):
+    def each_plane(plane, carry):
+        inverse_modes(modes_ref, kept_ref, plane)
+        for quarter in range(4):
+            places = []
+            for y in range(quarter * 4, quarter * 4 + 4):
+                for group in range(CL // 16):
+                    values = inverse_y(kept_ref, y, pl.ds(group * 16, 16))
+                    for at, (place, value) in enumerate(values.items()):
+                        if group == 0:
+                            places.append(place)
+                        high = value.astype(jnp.bfloat16)
+                        low = (value - high.astype(jnp.float32)).astype(jnp.bfloat16)
+                        rows = pl.ds(((y % 4) * 4 + at) * CL + group * 16, 16)
+                        even = jnp.concatenate([high[:, :64], low[:, :64]], axis=1)
+                        odd = jnp.concatenate([high[:, 64:], low[:, 64:]], axis=1)
+                        lhs_ref[quarter, rows, :LANES] = even
+                        lhs_ref[quarter, rows, LANES : 2 * LANES] = high
+                        lhs_ref[quarter, rows, 2 * LANES :] = odd
+            even = dot(lhs_ref[quarter, :, : 2 * LANES], table_ref[:, : ZT // 2])
+            odd = dot(lhs_ref[quarter, :, LANES:], table_ref[:, ZT // 2 :])
+            for at, y in enumerate(places):
+                part_even = even[at * CL : at * CL + CL]
+                part_odd = odd[at * CL : at * CL + CL]
+                sides = ((part_even + part_odd, 0), (part_even - part_odd, ZT // 2))
+                for scaled, first in sides:
+                    value = (ROOT_HALF * scaled) * (1.0 + lax.erf(scaled))
+                    cells = pl.ds(first, ZT // 2)
+                    out_ref[plane, y, :, cells] = (
+                        field_ref[plane, y, :, cells].astype(jnp.float32) + value
+                    )
+                pltpu.make_async_copy(out_ref.at[plane, y], out_hbm.at[plane, y], out_sem).start()
+        return carry
+
+    lax.fori_loop(0, XL, each_plane, 0)
+    pltpu.make_async_copy(out_ref, out_hbm, out_sem).wait()
+
+
+def inverse(*operands):
     return pl.pallas_call(
         inverse_kernel,
-        grid=(XL, GY // rows_y),
-        in_specs=[
-            pl.BlockSpec((SLABS * BLOCK, LANES), lambda x, y: (0, 0)),
-            pl.BlockSpec((1, rows_y, CL, ZT), lambda x, y: (x, y, 0, 0)),
-            pl.BlockSpec((3 * LANES, ZT), lambda x, y: (0, 0)),
-            pl.BlockSpec((1, CL), lambda x, y: (0, 0)),
-        ],
-        out_specs=pl.BlockSpec((1, rows_y, CL, ZT), lambda x, y: (x, y, 0, 0)),
+        in_specs=[pl.BlockSpec(memory_space=pltpu.VMEM)] * len(operands),
+        out_specs=pl.BlockSpec(memory_space=pl.ANY),
         out_shape=jax.ShapeDtypeStruct((XL, GY, CL, ZT), jnp.float32),
         scratch_shapes=[
-            pltpu.VMEM((GY * CL, 2 * LANES), jnp.bfloat16),
-            pltpu.VMEM((8, LANES), jnp.float32),
+            pltpu.VMEM((2, MY, CL, LANES), jnp.float32),
+            pltpu.VMEM((4, GY // 4 * CL, 3 * LANES), jnp.bfloat16),
+            pltpu.VMEM((XL, GY, CL, ZT), jnp.float32),
+            pltpu.SemaphoreType.DMA,
         ],
         compiler_params=pltpu.CompilerParams(vmem_limit_bytes=VMEM_LIMIT),
-    )(modes, field, table, bias)
+    )(*[pltpu.with_memory_space_constraint(operand, pltpu.VMEM) for operand in operands])
 
 
 def shards(field, spectral_weights, bias):
     weights = spectral_weights.reshape(2, QL * MX, MY * CL, LANES)
-    back = exchange(
+    modes, field_near, zt_back = exchange(
         field,
         weights,
         jnp.asarray(forward_zt_table()),
         jnp.asarray(forward_x_table()),
         jnp.asarray(inverse_x_table()),
+        jnp.asarray(inverse_zt_table()),
+        bias.reshape(1, CL),
     )
-    return inverse(back, field, jnp.asarray(inverse_zt_table()), bias.reshape(1, CL))
+    return inverse(modes, field_near, zt_back)
 
 
 def solution(mesh):

time: 38.3 us -> 31.7 us (0.83)
  Pallas kernels: 38 us -> 31.6 us
    pallas_call x2, Pallas kernels: 38 us -> 31.6 us  [the longest x1 27.2 us: exchange(): pl.pallas_call(exchange_kernel, in_specs=[pl.BlockSpec(memory_space=pl.AN...]
where the time goes in v2:
time: 31.7 us; the launch traced here: 31.6 us
  Pallas kernels  31.6 us (100%)
    pallas_call x1, Pallas kernels, exchange(): pl.pallas_call(exchange_kernel, in_specs=[pl.BlockSpec(memory_space=pl.AN...  27.2 us
    pallas_call x1, Pallas kernels, inverse(): pl.pallas_call(inverse_kernel, in_specs=[pl.BlockSpec(memory_space=pltpu....  4.37 us

profile of v2, /device:TPU:1, one launch (start us, length us, event | category | flops | bytes accessed | tf_op | source)
XLA Modules:
  0.0 31.6 jit_solution(6192146607840993735)
XLA Ops:
  0.0 27.2 %shard_map.73 = (f32[512,128]{1,0:T(8,128)S(1)}, bf16[2,64,32,512]{3,2,1,0:T(8,128)(2,1)S(1)}, bf16[256,512]{1,0:T(8,128)(2,1)S(1)}) custom-call(bf16[2,64,32,512]{3,2,1,0:T(8,128)(2,1)} %field_ref.1, f32[2,16,256,128]{3,2,1,0:T(8,128)} %bitcast.2, bf16[512,256]{1,0:T(8,128)(2,1)} %constant.8.clone.zt_hbm, f32[16,128]{1,0:T(8,128)} %constant.9.clone.x_forward_hbm, ...), custom_call_target="tpu_custom_call" | custom-call | tf_op jit(solution)/shard_map/pallas_call | solution.py:425
  27.2 4.4 %shard_map.74 = f32[2,64,32,512]{3,2,1,0:T(8,128)} custom-call(f32[512,128]{1,0:T(8,128)S(1)} %get-tuple-element.8.modes_ref, bf16[2,64,32,512]{3,2,1,0:T(8,128)(2,1)S(1)} %get-tuple-element.9.field_ref, bf16[256,512]{1,0:T(8,128)(2,1)S(1)} %get-tuple-element.10.table_ref), custom_call_target="tpu_custom_call" | custom-call | tf_op jit(solution)/shard_map/pallas_call | solution.py:552

commit v3 on v2

--- a/solution.py
+++ b/solution.py
@@ -18,7 +18,7 @@
 QL = KQ // SLABS
 CL = 32
 LANES = 128
-BLOCK = 16
+BLOCK = 8
 MESH = pl.DeviceIdType.MESH
 VMEM_LIMIT = 40 << 20
 CHUNKS = 2
@@ -120,47 +120,79 @@
     return jnp.where(lane % 64 < 32, -ahead, behind)
 
 
-def forward_y(modes_ref, kept_ref, out_ref, plane):
-    half = GY // 2
-    for group in range(CL // 8):
-        rows = pl.ds(group * 8, 8)
-
-        def load(y):
-            return modes_ref[y, rows, :]
-
-        first, middle = load(0), load(half)
-        even, odd = first + middle, first - middle
-        cosines = [even if k % 2 == 0 else odd for k in range(MY)]
-        first, middle = load(half // 2), load(half // 2 + half)
-        even, odd = first + middle, first - middle
-        sines = [None] * MY
-        for k in range(MY):
-            if k % 2 == 0:
-                cosines[k] = cosines[k] + (even if k % 4 == 0 else -even)
-            else:
-                sines[k] = odd if k % 4 == 1 else -odd
-        for y in range(1, half // 2):
-            a, b, c, d = load(y), load(GY - y), load(half - y), load(half + y)
-            sum1, dif1, sum2, dif2 = a + b, a - b, c + d, c - d
-            for_even, for_odd = sum1 + sum2, sum1 - sum2
-            sin_odd, sin_even = dif1 + dif2, dif1 - dif2
-            for k in range(MY):
-                cosines[k] = cosines[k] + cos_y(k, y) * (for_even if k % 2 == 0 else for_odd)
-                if k > 0:
-                    term = sin_y(k, y) * (sin_even if k % 2 == 0 else sin_odd)
-                    sines[k] = term if sines[k] is None else sines[k] + term
-        for k in range(MY):
-            value = cosines[k]
-            if k > 0:
-                value = value + rotate_forward(sines[k])
-            kept_ref[pl.ds(k * CL + group * 8, 8), :] = value
+def forward_y(modes_ref, kept_ref, group):
+    rows = pl.ds(group * 8, 8)
+    half, quarter = GY // 2, GY // 4
+    cosines, sines = [None] * MY, [None] * MY
+
+    def load(y):
+        return modes_ref[y, rows, :]
+
+    def add(sums, k, factor, value):
+        if factor == 1.0:
+            term = value
+        elif factor == -1.0:
+            term = -value
+        else:
+            term = factor * value
+        sums[k] = term if sums[k] is None else sums[k] + term
+
+    def fold(y):
+        a, b, c, d = load(y), load(GY - y), load(half - y), load(half + y)
+        sum1, dif1, sum2, dif2 = a + b, a - b, c + d, c - d
+        return sum1 + sum2, sum1 - sum2, dif1 - dif2, dif1 + dif2
+
+    first, middle = load(0), load(half)
+    low, high = load(quarter), load(quarter + half)
+    ends = first + middle
+    sides = low + high
+    for k in range(MY):
+        if k % 4 == 0:
+            add(cosines, k, 1.0, ends + sides)
+        elif k % 4 == 2:
+            add(cosines, k, 1.0, ends - sides)
+        else:
+            add(cosines, k, 1.0, first - middle)
+            add(sines, k, 1.0 if k % 4 == 1 else -1.0, low - high)
+    for y in range(1, quarter // 2 + 1):
+        pairs = [(y, fold(y))]
+        if y < quarter // 2:
+            pairs.append((quarter - y, fold(quarter - y)))
+        for at, (_, cos_odd, _, sin_odd) in pairs:
+            for k in range(1, MY, 2):
+                add(cosines, k, cos_y(k, at), cos_odd)
+                add(sines, k, sin_y(k, at), sin_odd)
+        cos_even, sin_even = pairs[0][1][0], pairs[0][1][2]
+        cos_sum = cos_dif = cos_even
+        sin_sum = sin_dif = sin_even
+        if len(pairs) > 1:
+            cos_more, sin_more = pairs[1][1][0], pairs[1][1][2]
+            cos_sum, cos_dif = cos_even + cos_more, cos_even - cos_more
+            sin_sum, sin_dif = sin_even + sin_more, sin_even - sin_more
+        add(cosines, 0, 1.0, cos_sum)
+        add(cosines, 4, cos_y(4, y), cos_sum)
+        for k in (2, 6):
+            if len(pairs) > 1:
+                add(cosines, k, cos_y(k, y), cos_dif)
+            add(sines, k, sin_y(k, y), sin_sum)
+        if len(pairs) > 1:
+            add(sines, 4, sin_y(4, y), sin_dif)
+    for k in range(MY):
+        value = cosines[k]
+        if k > 0:
+            value = value + rotate_forward(sines[k])
+        kept_ref[pl.ds(k * CL + group * 8, 8), :] = value
+
+
+def forward_turn(kept_ref, out_ref, plane):
     for ky_half in range(2):
         turned = kept_ref[pl.ds(ky_half * LANES, LANES), :].T
-        for part in range(4):
+        for at in range(4):
+            part, parity = at // 2, at % 2
             for owners in range(SLABS // 8):
-                start = owners * 8 * BLOCK + plane * 8 + ky_half * 4 + part
-                out_ref[pl.ds(start, 8, stride=BLOCK), :] = turned[
-                    part * SLABS + owners * 8 : part * SLABS + owners * 8 + 8
+                start = owners * 8 * BLOCK + plane * 4 + ky_half * 2 + part
+                out_ref[parity, pl.ds(start, 8, stride=BLOCK), :] = turned[
+                    at * SLABS + owners * 8 : at * SLABS + owners * 8 + 8
                 ]
 
 
@@ -180,8 +212,10 @@
     x_inverse_ref,
     bias_ref,
     shift_ref,
-    modes_ref,
-    kept_ref,
+    modes_even,
+    modes_odd,
+    kept_even,
+    kept_odd,
     ready_ref,
     arrived,
     staged,
@@ -200,11 +234,11 @@
     recv_sem,
     chan_send,
     chan_recv,
+    back_local,
     back_send,
     back_recv,
 ):
     slab, chan = lax.axis_index("slab"), lax.axis_index("chan")
-    highest = lax.Precision.HIGHEST
 
     def weight_copy(part):
         return pltpu.make_async_copy(weights_ref.at[part], staged.at[part], weight_sem.at[part])
@@ -257,28 +291,43 @@
     lax.fori_loop(1, CHANS, greet_chan, 0)
     table_copies[0].wait()
 
-    for plane in range(XL):
-        for piece in range(CHUNKS):
-            field_copy(plane, piece).wait()
-            rows = pl.ds(piece * chunk, chunk)
-            both = dot(field_in[plane, rows].reshape(chunk * CL, ZT), zt_ref[...])
-            both = both[:, :LANES] + both[:, LANES:]
-            modes_ref[rows] = both.reshape(chunk, CL, LANES)
-        forward_y(modes_ref, kept_ref, ready_ref, plane)
+    modes = (modes_even, modes_odd)
+    kept = (kept_even, kept_odd)
+
+    def forward_zt(plane, first, count):
+        rows = pl.ds(first, count)
+        both = dot(field_in[plane, rows].reshape(count * CL, ZT), zt_ref[...])
+        both = both[:, :LANES] + both[:, LANES:]
+        modes[plane][rows] = both.reshape(count, CL, LANES)
+
+    for piece in range(CHUNKS):
+        field_copy(0, piece).wait()
+        forward_zt(0, piece * chunk, chunk)
+    field_copy(1, 0).wait()
+    for group in range(CL // 8):
+        forward_zt(1, group * chunk // 4, chunk // 4)
+        forward_y(modes[0], kept[0], group)
+    forward_turn(kept[0], ready_ref, 0)
+    for piece in range(1, CHUNKS):
+        field_copy(1, piece).wait()
+        forward_zt(1, piece * chunk, chunk)
+    for group in range(CL // 8):
+        forward_y(modes[1], kept[1], group)
+    forward_turn(kept[1], ready_ref, 1)
 
     pl.semaphore_wait(barrier, SLABS + CHANS - 2)
 
     def block_of(owner):
         return pl.ds(pl.multiple_of(owner * BLOCK, BLOCK), BLOCK)
 
-    def send_all(source, target, place, send, recv):
+    def send_all(source, target, place, parity, local, send, recv):
         def step(i, carry):
             other = lax.rem(slab + i, SLABS)
             pltpu.make_async_remote_copy(
-                src_ref=source.at[block_of(other)],
-                dst_ref=target.at[block_of(place)],
-                send_sem=send,
-                recv_sem=recv,
+                src_ref=source.at[parity, block_of(other)],
+                dst_ref=target.at[parity, block_of(place)],
+                send_sem=send.at[parity],
+                recv_sem=recv.at[parity],
                 device_id=(other, chan),
                 device_id_type=MESH,
             ).start()
@@ -286,16 +335,19 @@
 
         lax.fori_loop(1, SLABS, step, 0)
         own = pltpu.make_async_copy(
-            source.at[block_of(slab)], target.at[block_of(place)], local_sem
+            source.at[parity, block_of(slab)], target.at[parity, block_of(place)], local.at[parity]
         )
         own.start()
         return own
 
-    def wait_bytes(ref, rows, sem):
-        piece = ref.at[pl.ds(0, rows)]
-        pltpu.make_async_copy(piece, piece, sem).wait()
-
-    own = send_all(ready_ref, arrived, slab, send_sem, recv_sem)
+    def wait_sent(ref, parity, sem):
+        piece = ref.at[parity, pl.ds(0, (SLABS - 1) * BLOCK)]
+        pltpu.make_async_copy(piece, piece, sem.at[parity]).wait()
+
+    owns = [
+        send_all(ready_ref, arrived, slab, parity, local_sem, send_sem, recv_sem)
+        for parity in range(QL)
+    ]
 
     for part in range(2):
         weight_copy(part).wait()
@@ -312,35 +364,33 @@
 
     for copy in table_copies[1:]:
         copy.wait()
-    own.wait()
-    rows_sent = (SLABS - 1) * BLOCK
-    wait_bytes(arrived, rows_sent, recv_sem)
-
-    columns = []
-    for parity in range(QL):
-        for ky_half in range(2):
-            columns.append(
-                jnp.concatenate(
-                    [
-                        arrived[pl.ds(ky_half * 4 + part * 2 + parity, GX, stride=8), :]
-                        for part in range(2)
-                    ],
-                    axis=0,
-                )
-            )
-    spectrum = dot(x_forward_ref[...], jnp.concatenate(columns, axis=1), highest)
-    for parity in range(QL):
-        spectrum_ref[parity] = spectrum[:, parity * 256 : (parity + 1) * 256]
-
     row = lax.broadcasted_iota(jnp.int32, (MY, 256), 0)
     lane = lax.broadcasted_iota(jnp.int32, (MY, 256), 1)
     own_ky = row == lane // CL
-
-    def mix(parity, carry):
+    out_lane = lax.broadcasted_iota(jnp.int32, (8, LANES), 1) // CL
+    chan_copies = []
+
+    for parity in range(QL):
+        owns[parity].wait()
+        wait_sent(arrived, parity, recv_sem)
+        columns = [
+            jnp.concatenate(
+                [
+                    arrived[parity, pl.ds(ky_half * 2 + part, GX, stride=4), :]
+                    for part in range(2)
+                ],
+                axis=0,
+            )
+            for ky_half in range(2)
+        ]
+        spectrum_ref[...] = dot(
+            x_forward_ref[...], jnp.concatenate(columns, axis=1), lax.Precision.HIGH
+        )
+
         for kx in range(MX):
             spread = jnp.concatenate(
                 [
-                    jnp.where(own_ky, spectrum_ref[parity, pl.ds(2 * kx + part, 1), :], 0.0)
+                    jnp.where(own_ky, spectrum_ref[pl.ds(2 * kx + part, 1), :], 0.0)
                     for part in range(2)
                 ],
                 axis=0,
@@ -350,22 +400,13 @@
             main = dot(jnp.concatenate([high, low], axis=0), high_ref[parity * MX + kx])
             rest = dot(high, low_ref[parity * MX + kx])
             both = main[:16] + main[16:] + rest
-            real = both[:8, :LANES] - both[8:, LANES:]
-            imag = both[:8, LANES:] + both[8:, :LANES]
-            partial_ref[pl.ds(parity * LANES + kx * 16, 8), :] = real
-            partial_ref[pl.ds(parity * LANES + kx * 16 + 8, 8), :] = imag
-        return carry
-
-    lax.fori_loop(0, QL, mix, 0)
-
-    lane = lax.broadcasted_iota(jnp.int32, (8, LANES), 1) // CL
-    for parity in range(QL):
+            partial_ref[pl.ds(kx * 16, 8), :] = both[:8, :LANES] - both[8:, LANES:]
+            partial_ref[pl.ds(kx * 16 + 8, 8), :] = both[:8, LANES:] + both[8:, :LANES]
+
         for ky_half in range(2):
             for rows in range(2):
                 pieces = [
-                    partial_ref[
-                        pl.ds(parity * LANES + rows * 64 + ky_half * 4 + ky, 8, stride=8), :
-                    ]
+                    partial_ref[pl.ds(rows * 64 + ky_half * 4 + ky, 8, stride=8), :]
                     for ky in range(4)
                 ]
                 for other in range(CHANS):
@@ -373,61 +414,67 @@
                     for ky in range(4):
                         shift = (ky - other) % CHANS * CL
                         moved = pltpu.roll(pieces[ky], shift, 1) if shift else pieces[ky]
-                        packed = moved if packed is None else jnp.where(lane == ky, moved, packed)
-                    start = (parity * 2 + ky_half) * 16 + rows * 8
-                    parcels[other, pl.ds(start, 8), :] = packed
-
-    chan_copies = []
-    for i in range(1, CHANS):
-        other = lax.rem(chan + i, CHANS)
-        copy = pltpu.make_async_remote_copy(
-            src_ref=parcels.at[other],
-            dst_ref=parcels_in.at[i - 1],
-            send_sem=chan_send.at[i - 1],
-            recv_sem=chan_recv.at[i - 1],
-            device_id=(slab, other),
-            device_id_type=MESH,
-        )
-        copy.start()
-        chan_copies.append(copy)
-    mixed = parcels[chan]
-    for i in range(1, CHANS):
-        chan_copies[i - 1].wait_recv()
-        mixed = mixed + parcels_in[i - 1]
+                        packed = (
+                            moved if packed is None else jnp.where(out_lane == ky, moved, packed)
+                        )
+                    parcels[parity, other, pl.ds(ky_half * 16 + rows * 8, 8), :] = packed
+
+        copies = []
+        for i in range(1, CHANS):
+            other = lax.rem(chan + i, CHANS)
+            copy = pltpu.make_async_remote_copy(
+                src_ref=parcels.at[parity, other],
+                dst_ref=parcels_in.at[parity, i - 1],
+                send_sem=chan_send.at[parity, i - 1],
+                recv_sem=chan_recv.at[parity, i - 1],
+                device_id=(slab, other),
+                device_id_type=MESH,
+            )
+            copy.start()
+            copies.append(copy)
+        chan_copies.append(copies)
 
     shift_ref[...] = jnp.zeros_like(shift_ref)
     shift_ref[0:1, :CL] = bias_ref[...] * DC_SCALE
-    shift = jnp.where(slab == 0, shift_ref[...], 0.0)
-    mixed = jnp.concatenate([mixed[:8] + shift, mixed[8:]], axis=0)
-
-    side = jnp.concatenate([mixed[16 * i : 16 * i + 16] for i in range(4)], axis=1)
-    spatial = dot(x_inverse_ref[...], side, highest)
+    bias_shift = jnp.where(slab == 0, shift_ref[...], 0.0)
+    place = slab // 4 % 2 * 16 + slab // 8 * 4 + slab % 4
+    owns = []
+
     for parity in range(QL):
+        mixed = parcels[parity, chan]
+        for i in range(1, CHANS):
+            chan_copies[parity][i - 1].wait_recv()
+            mixed = mixed + parcels_in[parity, i - 1]
+        if parity == 0:
+            mixed = jnp.concatenate([mixed[:8] + bias_shift, mixed[8:]], axis=0)
+        side = jnp.concatenate([mixed[:16], mixed[16:]], axis=1)
+        spatial = dot(x_inverse_ref[...], side, lax.Precision.HIGH)
         for ky_half in range(2):
             for part in range(2):
-                at = parity * 2 + ky_half
-                outgoing[pl.ds(ky_half * 4 + part * 2 + parity, GX, stride=8), :] = spatial[
-                    part * GX : (part + 1) * GX, at * LANES : (at + 1) * LANES
+                outgoing[parity, pl.ds(ky_half * 2 + part, GX, stride=4), :] = spatial[
+                    part * GX : (part + 1) * GX, ky_half * LANES : (ky_half + 1) * LANES
                 ]
-
-    place = slab // 4 % 2 * 16 + slab // 8 * 4 + slab % 4
-    own = send_all(outgoing, out_ref, place, back_send, back_recv)
-    own.wait()
-    for copy in chan_copies:
-        copy.wait_send()
-    wait_bytes(ready_ref, rows_sent, send_sem)
-    wait_bytes(out_ref, rows_sent, back_recv)
-    wait_bytes(outgoing, rows_sent, back_send)
+        owns.append(
+            send_all(outgoing, out_ref, place, parity, back_local, back_send, back_recv)
+        )
+
+    for parity in range(QL):
+        owns[parity].wait()
+        for copy in chan_copies[parity]:
+            copy.wait_send()
+        wait_sent(ready_ref, parity, send_sem)
+        wait_sent(out_ref, parity, back_recv)
+        wait_sent(outgoing, parity, back_send)
 
 
 def exchange(*operands):
-    rows = SLABS * BLOCK
+    blocks = (QL, SLABS * BLOCK, LANES)
     return pl.pallas_call(
         exchange_kernel,
         in_specs=[pl.BlockSpec(memory_space=pl.ANY)] * len(operands),
         out_specs=[pl.BlockSpec(memory_space=pltpu.VMEM)] * 3,
         out_shape=[
-            pltpu.VMEM((rows, LANES), jnp.float32),
+            pltpu.VMEM(blocks, jnp.float32),
             pltpu.VMEM((XL, GY, CL, ZT), jnp.bfloat16),
             pltpu.VMEM((2 * LANES, ZT), jnp.bfloat16),
         ],
@@ -438,27 +485,30 @@
             pltpu.VMEM((1, CL), jnp.float32),
             pltpu.VMEM((8, LANES), jnp.float32),
             pltpu.VMEM((GY, CL, LANES), jnp.float32),
+            pltpu.VMEM((GY, CL, LANES), jnp.float32),
             pltpu.VMEM((MY * CL, LANES), jnp.float32),
-            pltpu.VMEM((rows, LANES), jnp.float32),
-            pltpu.VMEM((rows, LANES), jnp.float32),
+            pltpu.VMEM((MY * CL, LANES), jnp.float32),
+            pltpu.VMEM(blocks, jnp.float32),
+            pltpu.VMEM(blocks, jnp.float32),
             pltpu.VMEM((2, QL * MX, 256, LANES), jnp.float32),
             pltpu.VMEM((QL * MX, 256, 256), jnp.bfloat16),
             pltpu.VMEM((QL * MX, 256, 256), jnp.bfloat16),
-            pltpu.VMEM((QL, 16, 256), jnp.float32),
-            pltpu.VMEM((QL * LANES, LANES), jnp.float32),
-            pltpu.VMEM((CHANS, 64, LANES), jnp.float32),
-            pltpu.VMEM((CHANS - 1, 64, LANES), jnp.float32),
-            pltpu.VMEM((rows, LANES), jnp.float32),
+            pltpu.VMEM((16, 256), jnp.float32),
+            pltpu.VMEM((LANES, LANES), jnp.float32),
+            pltpu.VMEM((QL, CHANS, 32, LANES), jnp.float32),
+            pltpu.VMEM((QL, CHANS - 1, 32, LANES), jnp.float32),
+            pltpu.VMEM(blocks, jnp.float32),
             pltpu.SemaphoreType.DMA((5,)),
             pltpu.SemaphoreType.DMA((XL, CHUNKS)),
             pltpu.SemaphoreType.DMA((2,)),
-            pltpu.SemaphoreType.DMA,
-            pltpu.SemaphoreType.DMA,
-            pltpu.SemaphoreType.DMA,
-            pltpu.SemaphoreType.DMA((CHANS - 1,)),
-            pltpu.SemaphoreType.DMA((CHANS - 1,)),
-            pltpu.SemaphoreType.DMA,
-            pltpu.SemaphoreType.DMA,
+            pltpu.SemaphoreType.DMA((QL,)),
+            pltpu.SemaphoreType.DMA((QL,)),
+            pltpu.SemaphoreType.DMA((QL,)),
+            pltpu.SemaphoreType.DMA((QL, CHANS - 1)),
+            pltpu.SemaphoreType.DMA((QL, CHANS - 1)),
+            pltpu.SemaphoreType.DMA((QL,)),
+            pltpu.SemaphoreType.DMA((QL,)),
+            pltpu.SemaphoreType.DMA((QL,)),
         ],
         compiler_params=pltpu.CompilerParams(
             collective_id=0, has_side_effects=True, vmem_limit_bytes=VMEM_LIMIT
@@ -471,10 +521,13 @@
         piece = jnp.concatenate(
             [
                 modes_ref[
-                    pl.ds(odd * (16 * BLOCK) + plane * 8 + ky_half * 4 + part, 16, stride=BLOCK), :
+                    parity,
+                    pl.ds(odd * (16 * BLOCK) + plane * 4 + ky_half * 2 + part, 16, stride=BLOCK),
+                    :,
                 ]
                 for odd in range(2)
-                for part in range(4)
+                for part in range(2)
+                for parity in range(2)
             ],
             axis=0,
         )

time: 31.7 us -> 30.6 us (0.965)
  Pallas kernels: 31.6 us -> 30.5 us
    pallas_call x1, Pallas kernels: 27.2 us -> 26.1 us  [exchange(): pl.pallas_call(exchange_kernel, in_specs=[pl.BlockSpec(memory_space=pl.AN...]
where the time goes in v3:
time: 30.6 us; the launch traced here: 30.5 us
  Pallas kernels  30.5 us (100%)
    pallas_call x1, Pallas kernels, exchange(): pl.pallas_call(exchange_kernel, in_specs=[pl.BlockSpec(memory_space=pl.AN...  26.1 us
    pallas_call x1, Pallas kernels, inverse(): pl.pallas_call(inverse_kernel, in_specs=[pl.BlockSpec(memory_space=pltpu....  4.37 us

profile of v3, /device:TPU:1, one launch (start us, length us, event | category | flops | bytes accessed | tf_op | source)
XLA Modules:
  0.0 30.5 jit_solution(17350587390137322929)
XLA Ops:
  0.0 26.1 %shard_map.73 = (f32[2,256,128]{2,1,0:T(8,128)S(1)}, bf16[2,64,32,512]{3,2,1,0:T(8,128)(2,1)S(1)}, bf16[256,512]{1,0:T(8,128)(2,1)S(1)}) custom-call(bf16[2,64,32,512]{3,2,1,0:T(8,128)(2,1)} %field_ref.1, f32[2,16,256,128]{3,2,1,0:T(8,128)} %bitcast.2, bf16[512,256]{1,0:T(8,128)(2,1)} %constant.8.clone.zt_hbm, f32[16,128]{1,0:T(8,128)} %constant.9.clone.x_forward_hbm, ...), custom_call_target="tpu_custom_call" | custom-call | tf_op jit(solution)/shard_map/pallas_call | solution.py:472
  26.1 4.4 %shard_map.74 = f32[2,64,32,512]{3,2,1,0:T(8,128)} custom-call(f32[2,256,128]{2,1,0:T(8,128)S(1)} %get-tuple-element.8.modes_ref, bf16[2,64,32,512]{3,2,1,0:T(8,128)(2,1)S(1)} %get-tuple-element.9.field_ref, bf16[256,512]{1,0:T(8,128)(2,1)S(1)} %get-tuple-element.10.table_ref), custom_call_target="tpu_custom_call" | custom-call | tf_op jit(solution)/shard_map/pallas_call | solution.py:605

commit v4 on v3

--- a/solution.py
+++ b/solution.py
@@ -25,6 +25,12 @@
 
 DC_SCALE = float(GX * GY * GZ * GT)
 ROOT_HALF = math.sqrt(0.5)
+
+
+FAR_FIRST = sorted(
+    [(z, y, c) for z in range(4) for y in range(4) for c in range(2) if (z, y, c) != (0, 0, 0)],
+    key=lambda step: -min(step[0], 4 - step[0]) - min(step[1], 4 - step[1]),
+)
 
 
 def split_bf16(table):
@@ -205,8 +211,9 @@
     zt_back_hbm,
     bias_hbm,
     out_ref,
+    field_wide,
+    zt_back_ref,
     field_in,
-    zt_back_ref,
     zt_ref,
     x_forward_ref,
     x_inverse_ref,
@@ -269,9 +276,6 @@
             field_copy(plane, piece).start()
     for copy in table_copies[1:4]:
         copy.start()
-    for part in range(2):
-        weight_copy(part).start()
-    table_copies[4].start()
 
     barrier = pltpu.get_barrier_semaphore()
 
@@ -310,6 +314,10 @@
     forward_turn(kept[0], ready_ref, 0)
     for piece in range(1, CHUNKS):
         field_copy(1, piece).wait()
+        if piece == CHUNKS - 1:
+            for part in range(2):
+                weight_copy(part).start()
+            table_copies[4].start()
         forward_zt(1, piece * chunk, chunk)
     for group in range(CL // 8):
         forward_y(modes[1], kept[1], group)
@@ -317,12 +325,22 @@
 
     pl.semaphore_wait(barrier, SLABS + CHANS - 2)
 
+    def wrapped(position, size):
+        ahead = [position + step for step in range(size)]
+        return [jnp.where(at >= size, at - size, at) for at in ahead]
+
+    z = lax.div(slab, 8)
+    y = lax.div(slab - z * 8, 2)
+    at_z = [at * 8 for at in wrapped(z, 4)]
+    at_y = [at * 2 for at in wrapped(y, 4)]
+    at_core = wrapped(slab - z * 8 - y * 2, 2)
+
     def block_of(owner):
         return pl.ds(pl.multiple_of(owner * BLOCK, BLOCK), BLOCK)
 
     def send_all(source, target, place, parity, local, send, recv):
-        def step(i, carry):
-            other = lax.rem(slab + i, SLABS)
+        for dz, dy, dc in FAR_FIRST:
+            other = at_z[dz] + at_y[dy] + at_core[dc]
             pltpu.make_async_remote_copy(
                 src_ref=source.at[parity, block_of(other)],
                 dst_ref=target.at[parity, block_of(place)],
@@ -331,9 +349,6 @@
                 device_id=(other, chan),
                 device_id_type=MESH,
             ).start()
-            return carry
-
-        lax.fori_loop(1, SLABS, step, 0)
         own = pltpu.make_async_copy(
             source.at[parity, block_of(slab)], target.at[parity, block_of(place)], local.at[parity]
         )
@@ -361,6 +376,12 @@
             return carry
 
         lax.fori_loop(0, QL * MX, split_weights, 0)
+
+    def widen(i, carry):
+        field_wide[i // GY, i % GY] = field_in[i // GY, i % GY].astype(jnp.float32)
+        return carry
+
+    lax.fori_loop(0, XL * GY, widen, 0)
 
     for copy in table_copies[1:]:
         copy.wait()
@@ -420,7 +441,7 @@
                     parcels[parity, other, pl.ds(ky_half * 16 + rows * 8, 8), :] = packed
 
         copies = []
-        for i in range(1, CHANS):
+        for i in (2, 1, 3):
             other = lax.rem(chan + i, CHANS)
             copy = pltpu.make_async_remote_copy(
                 src_ref=parcels.at[parity, other],
@@ -432,7 +453,7 @@
             )
             copy.start()
             copies.append(copy)
-        chan_copies.append(copies)
+        chan_copies.append([copies[1], copies[0], copies[2]])
 
     shift_ref[...] = jnp.zeros_like(shift_ref)
     shift_ref[0:1, :CL] = bias_ref[...] * DC_SCALE
@@ -475,10 +496,11 @@
         out_specs=[pl.BlockSpec(memory_space=pltpu.VMEM)] * 3,
         out_shape=[
             pltpu.VMEM(blocks, jnp.float32),
-            pltpu.VMEM((XL, GY, CL, ZT), jnp.bfloat16),
+            pltpu.VMEM((XL, GY, CL, ZT), jnp.float32),
             pltpu.VMEM((2 * LANES, ZT), jnp.bfloat16),
         ],
         scratch_shapes=[
+            pltpu.VMEM((XL, GY, CL, ZT), jnp.bfloat16),
             pltpu.VMEM((ZT, 2 * LANES), jnp.bfloat16),
             pltpu.VMEM((2 * MX, 2 * GX), jnp.float32),
             pltpu.VMEM((2 * GX, 2 * MX), jnp.float32),
@@ -541,26 +563,36 @@
 def inverse_y(kept_ref, y, rows):
     kept = [kept_ref[0, k, rows, :] for k in range(MY)]
     spun = [kept_ref[1, k, rows, :] for k in range(MY)]
-    half = GY // 2
+    half, quarter = GY // 2, GY // 4
     if y == 0:
         even, odd = total(kept[0::2]), total(kept[1::2])
         values = {0: even + odd, half: even - odd}
         even = (kept[0] + kept[4]) - (kept[2] + kept[6])
         odd = (spun[1] + spun[5]) - (spun[3] + spun[7])
-        values.update({half // 2: even + odd, half // 2 + half: even - odd})
+        values.update({quarter: even + odd, quarter + half: even - odd})
         return values
-    cos_even = total([kept[0]] + [cos_y(k, y) * kept[k] for k in (2, 4, 6)])
-    cos_odd = total([cos_y(k, y) * kept[k] for k in (1, 3, 5, 7)])
-    sin_even = total([sin_y(k, y) * spun[k] for k in (2, 4, 6)])
-    sin_odd = total([sin_y(k, y) * spun[k] for k in (1, 3, 5, 7)])
-    cos_sum, cos_dif = cos_even + cos_odd, cos_even - cos_odd
-    sin_sum, sin_dif = sin_even + sin_odd, sin_odd - sin_even
-    return {
-        y: cos_sum + sin_sum,
-        GY - y: cos_sum - sin_sum,
-        half - y: cos_dif + sin_dif,
-        half + y: cos_dif - sin_dif,
-    }
+    values = {}
+
+    def put(at, cos_even, sin_even):
+        cos_odd = total([cos_y(k, at) * kept[k] for k in (1, 3, 5, 7)])
+        sin_odd = total([sin_y(k, at) * spun[k] for k in (1, 3, 5, 7)])
+        cos_sum, cos_dif = cos_even + cos_odd, cos_even - cos_odd
+        sin_sum, sin_dif = sin_even + sin_odd, sin_odd - sin_even
+        values[at] = cos_sum + sin_sum
+        values[GY - at] = cos_sum - sin_sum
+        values[half - at] = cos_dif + sin_dif
+        values[half + at] = cos_dif - sin_dif
+
+    if 2 * y == quarter:
+        put(y, kept[0] - kept[4], spun[2] - spun[6])
+        return values
+    cos_same = kept[0] + cos_y(4, y) * kept[4]
+    cos_turn = cos_y(2, y) * kept[2] + cos_y(6, y) * kept[6]
+    sin_same = sin_y(2, y) * spun[2] + sin_y(6, y) * spun[6]
+    sin_turn = sin_y(4, y) * spun[4]
+    put(y, cos_same + cos_turn, sin_same + sin_turn)
+    put(quarter - y, cos_same - cos_turn, sin_same - sin_turn)
+    return values
 
 
 def inverse_kernel(modes_ref, field_ref, table_ref, out_hbm, kept_ref, lhs_ref, out_ref, out_sem):
@@ -568,15 +600,16 @@
         inverse_modes(modes_ref, kept_ref, plane)
         for quarter in range(4):
             places = []
-            for y in range(quarter * 4, quarter * 4 + 4):
+            for y in ((1, 2), (3, 4), (5, 6), (7, 8, 0))[quarter]:
+                first = len(places)
                 for group in range(CL // 16):
                     values = inverse_y(kept_ref, y, pl.ds(group * 16, 16))
-                    for at, (place, value) in enumerate(values.items()):
-                        if group == 0:
-                            places.append(place)
+                    if group == 0:
+                        places += values
+                    for at, value in enumerate(values.values()):
                         high = value.astype(jnp.bfloat16)
                         low = (value - high.astype(jnp.float32)).astype(jnp.bfloat16)
-                        rows = pl.ds(((y % 4) * 4 + at) * CL + group * 16, 16)
+                        rows = pl.ds((first + at) * CL + group * 16, 16)
                         even = jnp.concatenate([high[:, :64], low[:, :64]], axis=1)
                         odd = jnp.concatenate([high[:, 64:], low[:, 64:]], axis=1)
                         lhs_ref[quarter, rows, :LANES] = even
@@ -588,11 +621,11 @@
                 part_even = even[at * CL : at * CL + CL]
                 part_odd = odd[at * CL : at * CL + CL]
                 sides = ((part_even + part_odd, 0), (part_even - part_odd, ZT // 2))
-                for scaled, first in sides:
+                for scaled, start in sides:
                     value = (ROOT_HALF * scaled) * (1.0 + lax.erf(scaled))
-                    cells = pl.ds(first, ZT // 2)
+                    cells = pl.ds(start, ZT // 2)
                     out_ref[plane, y, :, cells] = (
-                        field_ref[plane, y, :, cells].astype(jnp.float32) + value
+                        field_ref[plane, y, :, cells] + value
                     )
                 pltpu.make_async_copy(out_ref.at[plane, y], out_hbm.at[plane, y], out_sem).start()
         return carry

time: 30.6 us -> 29.8 us (0.974)
  Pallas kernels: 30.5 us -> 29.7 us
    pallas_call x1, Pallas kernels: 26.1 us -> 25.6 us  [exchange(): pl.pallas_call(exchange_kernel, in_specs=[pl.BlockSpec(memory_space=pl.AN...]
where the time goes in v4:
time: 29.8 us; the launch traced here: 29.7 us
  Pallas kernels  29.7 us (100%)
    pallas_call x1, Pallas kernels, exchange(): pl.pallas_call(exchange_kernel, in_specs=[pl.BlockSpec(memory_space=pl.AN...  25.6 us
    pallas_call x1, Pallas kernels, inverse(): pl.pallas_call(inverse_kernel, in_specs=[pl.BlockSpec(memory_space=pltpu....  4.1 us

profile of v4, /device:TPU:1, one launch (start us, length us, event | category | flops | bytes accessed | tf_op | source)
XLA Modules:
  0.0 29.7 jit_solution(6788035801064997180)
XLA Ops:
  0.0 25.6 %shard_map.73 = (f32[2,256,128]{2,1,0:T(8,128)S(1)}, f32[2,64,32,512]{3,2,1,0:T(8,128)S(1)}, bf16[256,512]{1,0:T(8,128)(2,1)S(1)}) custom-call(bf16[2,64,32,512]{3,2,1,0:T(8,128)(2,1)} %field_ref.1, f32[2,16,256,128]{3,2,1,0:T(8,128)} %bitcast.2, bf16[512,256]{1,0:T(8,128)(2,1)} %constant.8.clone.zt_hbm, f32[16,128]{1,0:T(8,128)} %constant.9.clone.x_forward_hbm, ...), custom_call_target="tpu_custom_call" | custom-call | tf_op jit(solution)/shard_map/pallas_call | solution.py:493
  25.6 4.1 %shard_map.74 = f32[2,64,32,512]{3,2,1,0:T(8,128)} custom-call(f32[2,256,128]{2,1,0:T(8,128)S(1)} %get-tuple-element.8.modes_ref, f32[2,64,32,512]{3,2,1,0:T(8,128)S(1)} %get-tuple-element.9.field_ref, bf16[256,512]{1,0:T(8,128)(2,1)S(1)} %get-tuple-element.10.table_ref), custom_call_target="tpu_custom_call" | custom-call | tf_op jit(solution)/shard_map/pallas_call | solution.py:638

commit v5 on v4

--- a/solution.py
+++ b/solution.py
@@ -21,7 +21,7 @@
 BLOCK = 8
 MESH = pl.DeviceIdType.MESH
 VMEM_LIMIT = 40 << 20
-CHUNKS = 2
+HALF = CL // 2
 
 DC_SCALE = float(GX * GY * GZ * GT)
 ROOT_HALF = math.sqrt(0.5)
@@ -250,12 +250,10 @@
     def weight_copy(part):
         return pltpu.make_async_copy(weights_ref.at[part], staged.at[part], weight_sem.at[part])
 
-    chunk = GY // CHUNKS
-
     def field_copy(plane, piece):
-        rows = pl.ds(piece * chunk, chunk)
+        rows = pl.ds(piece * HALF, HALF)
         return pltpu.make_async_copy(
-            field_ref.at[plane, rows], field_in.at[plane, rows], field_sem.at[plane, piece]
+            field_ref.at[plane, :, rows], field_in.at[plane, :, rows], field_sem.at[plane, piece]
         )
 
     table_copies = [
@@ -272,7 +270,7 @@
     ]
     table_copies[0].start()
     for plane in range(XL):
-        for piece in range(CHUNKS):
+        for piece in range(2):
             field_copy(plane, piece).start()
     for copy in table_copies[1:4]:
         copy.start()
@@ -298,29 +296,28 @@
     modes = (modes_even, modes_odd)
     kept = (kept_even, kept_odd)
 
-    def forward_zt(plane, first, count):
-        rows = pl.ds(first, count)
-        both = dot(field_in[plane, rows].reshape(count * CL, ZT), zt_ref[...])
+    def forward_zt(plane, piece, first, count):
+        at = (pl.ds(first, count), pl.ds(piece * HALF, HALF))
+        both = dot(field_in[plane, *at].reshape(count * HALF, ZT), zt_ref[...])
         both = both[:, :LANES] + both[:, LANES:]
-        modes[plane][rows] = both.reshape(count, CL, LANES)
-
-    for piece in range(CHUNKS):
-        field_copy(0, piece).wait()
-        forward_zt(0, piece * chunk, chunk)
-    field_copy(1, 0).wait()
-    for group in range(CL // 8):
-        forward_zt(1, group * chunk // 4, chunk // 4)
-        forward_y(modes[0], kept[0], group)
-    forward_turn(kept[0], ready_ref, 0)
-    for piece in range(1, CHUNKS):
-        field_copy(1, piece).wait()
-        if piece == CHUNKS - 1:
+        modes[plane][at] = both.reshape(count, HALF, LANES)
+
+    pieces = [(plane, piece) for plane in range(XL) for piece in range(2)]
+    for at, (plane, piece) in enumerate(pieces):
+        field_copy(plane, piece).wait()
+        if at == len(pieces) - 1:
             for part in range(2):
                 weight_copy(part).start()
             table_copies[4].start()
-        forward_zt(1, piece * chunk, chunk)
-    for group in range(CL // 8):
-        forward_y(modes[1], kept[1], group)
+        for part in range(2):
+            forward_zt(plane, piece, part * (GY // 2), GY // 2)
+            if at > 0:
+                before, group = pieces[at - 1][0], pieces[at - 1][1] * 2 + part
+                forward_y(modes[before], kept[before], group)
+        if at == 2:
+            forward_turn(kept[0], ready_ref, 0)
+    for part in range(2):
+        forward_y(modes[1], kept[1], 2 + part)
     forward_turn(kept[1], ready_ref, 1)
 
     pl.semaphore_wait(barrier, SLABS + CHANS - 2)
@@ -521,7 +518,7 @@
             pltpu.VMEM((QL, CHANS - 1, 32, LANES), jnp.float32),
             pltpu.VMEM(blocks, jnp.float32),
             pltpu.SemaphoreType.DMA((5,)),
-            pltpu.SemaphoreType.DMA((XL, CHUNKS)),
+            pltpu.SemaphoreType.DMA((XL, 2)),
             pltpu.SemaphoreType.DMA((2,)),
             pltpu.SemaphoreType.DMA((QL,)),
             pltpu.SemaphoreType.DMA((QL,)),

time: 29.8 us -> 29 us (0.973)
  Pallas kernels: 29.7 us -> 28.9 us
    pallas_call x1, Pallas kernels: 25.6 us -> 24.8 us  [exchange(): pl.pallas_call(exchange_kernel, in_specs=[pl.BlockSpec(memory_space=pl.AN...]
where the time goes in v5:
time: 29 us; the launch traced here: 28.9 us
  Pallas kernels  28.9 us (100%)
    pallas_call x1, Pallas kernels, exchange(): pl.pallas_call(exchange_kernel, in_specs=[pl.BlockSpec(memory_space=pl.AN...  24.8 us
    pallas_call x1, Pallas kernels, inverse(): pl.pallas_call(inverse_kernel, in_specs=[pl.BlockSpec(memory_space=pltpu....  4.1 us

profile of v5, /device:TPU:1, one launch (start us, length us, event | category | flops | bytes accessed | tf_op | source)
XLA Modules:
  0.0 28.9 jit_solution(7326680681246028141)
XLA Ops:
  0.0 24.8 %shard_map.73 = (f32[2,256,128]{2,1,0:T(8,128)S(1)}, f32[2,64,32,512]{3,2,1,0:T(8,128)S(1)}, bf16[256,512]{1,0:T(8,128)(2,1)S(1)}) custom-call(bf16[2,64,32,512]{3,2,1,0:T(8,128)(2,1)} %field_ref.1, f32[2,16,256,128]{3,2,1,0:T(8,128)} %bitcast.2, bf16[512,256]{1,0:T(8,128)(2,1)} %constant.8.clone.zt_hbm, f32[16,128]{1,0:T(8,128)} %constant.9.clone.x_forward_hbm, ...), custom_call_target="tpu_custom_call" | custom-call | tf_op jit(solution)/shard_map/pallas_call | solution.py:490
  24.8 4.1 %shard_map.74 = f32[2,64,32,512]{3,2,1,0:T(8,128)} custom-call(f32[2,256,128]{2,1,0:T(8,128)S(1)} %get-tuple-element.8.modes_ref, f32[2,64,32,512]{3,2,1,0:T(8,128)S(1)} %get-tuple-element.9.field_ref, bf16[256,512]{1,0:T(8,128)(2,1)S(1)} %get-tuple-element.10.table_ref), custom_call_target="tpu_custom_call" | custom-call | tf_op jit(solution)/shard_map/pallas_call | solution.py:635

commit v6 on v5

--- a/solution.py
+++ b/solution.py
@@ -361,6 +361,14 @@
         for parity in range(QL)
     ]
 
+    def widen(plane):
+        def step(i, carry):
+            field_wide[plane, i] = field_in[plane, i].astype(jnp.float32)
+            return carry
+
+        lax.fori_loop(0, GY, step, 0)
+
+    widen(0)
     for part in range(2):
         weight_copy(part).wait()
 
@@ -373,12 +381,6 @@
             return carry
 
         lax.fori_loop(0, QL * MX, split_weights, 0)
-
-    def widen(i, carry):
-        field_wide[i // GY, i % GY] = field_in[i // GY, i % GY].astype(jnp.float32)
-        return carry
-
-    lax.fori_loop(0, XL * GY, widen, 0)
 
     for copy in table_copies[1:]:
         copy.wait()
@@ -451,6 +453,8 @@
             copy.start()
             copies.append(copy)
         chan_copies.append([copies[1], copies[0], copies[2]])
+
+    widen(1)
 
     shift_ref[...] = jnp.zeros_like(shift_ref)
     shift_ref[0:1, :CL] = bias_ref[...] * DC_SCALE

time: 29 us -> 29 us (level)
  no operation moved by 1% of the time
where the time goes in v6:
time: 29 us; the launch traced here: 28.9 us
  Pallas kernels  28.9 us (100%)
    pallas_call x1, Pallas kernels, exchange(): pl.pallas_call(exchange_kernel, in_specs=[pl.BlockSpec(memory_space=pl.AN...  24.8 us
    pallas_call x1, Pallas kernels, inverse(): pl.pallas_call(inverse_kernel, in_specs=[pl.BlockSpec(memory_space=pltpu....  4.1 us

profile of v6, /device:TPU:1, one launch (start us, length us, event | category | flops | bytes accessed | tf_op | source)
XLA Modules:
  0.0 28.9 jit_solution(7064216917652028204)
XLA Ops:
  0.0 24.8 %shard_map.73 = (f32[2,256,128]{2,1,0:T(8,128)S(1)}, f32[2,64,32,512]{3,2,1,0:T(8,128)S(1)}, bf16[256,512]{1,0:T(8,128)(2,1)S(1)}) custom-call(bf16[2,64,32,512]{3,2,1,0:T(8,128)(2,1)} %field_ref.1, f32[2,16,256,128]{3,2,1,0:T(8,128)} %bitcast.2, bf16[512,256]{1,0:T(8,128)(2,1)} %constant.8.clone.zt_hbm, f32[16,128]{1,0:T(8,128)} %constant.9.clone.x_forward_hbm, ...), custom_call_target="tpu_custom_call" | custom-call | tf_op jit(solution)/shard_map/pallas_call | solution.py:494
  24.8 4.1 %shard_map.74 = f32[2,64,32,512]{3,2,1,0:T(8,128)} custom-call(f32[2,256,128]{2,1,0:T(8,128)S(1)} %get-tuple-element.8.modes_ref, f32[2,64,32,512]{3,2,1,0:T(8,128)S(1)} %get-tuple-element.9.field_ref, bf16[256,512]{1,0:T(8,128)(2,1)S(1)} %get-tuple-element.10.table_ref), custom_call_target="tpu_custom_call" | custom-call | tf_op jit(solution)/shard_map/pallas_call | solution.py:639

commit v7 on v6

--- a/solution.py
+++ b/solution.py
@@ -277,11 +277,15 @@
 
     barrier = pltpu.get_barrier_semaphore()
 
-    def greet_slab(i, carry):
-        pl.semaphore_signal(
-            barrier, inc=1, device_id=(lax.rem(slab + i, SLABS), chan), device_id_type=MESH
-        )
-        return carry
+    def wrapped(position, size):
+        ahead = [position + step for step in range(size)]
+        return [jnp.where(at >= size, at - size, at) for at in ahead]
+
+    z = lax.div(slab, 8)
+    y = lax.div(slab - z * 8, 2)
+    at_z = [at * 8 for at in wrapped(z, 4)]
+    at_y = [at * 2 for at in wrapped(y, 4)]
+    at_core = wrapped(slab - z * 8 - y * 2, 2)
 
     def greet_chan(i, carry):
         pl.semaphore_signal(
@@ -289,7 +293,9 @@
         )
         return carry
 
-    lax.fori_loop(1, SLABS, greet_slab, 0)
+    for dz, dy, dc in FAR_FIRST:
+        other = at_z[dz] + at_y[dy] + at_core[dc]
+        pl.semaphore_signal(barrier, inc=1, device_id=(other, chan), device_id_type=MESH)
     lax.fori_loop(1, CHANS, greet_chan, 0)
     table_copies[0].wait()
 
@@ -321,16 +327,6 @@
     forward_turn(kept[1], ready_ref, 1)
 
     pl.semaphore_wait(barrier, SLABS + CHANS - 2)
-
-    def wrapped(position, size):
-        ahead = [position + step for step in range(size)]
-        return [jnp.where(at >= size, at - size, at) for at in ahead]
-
-    z = lax.div(slab, 8)
-    y = lax.div(slab - z * 8, 2)
-    at_z = [at * 8 for at in wrapped(z, 4)]
-    at_y = [at * 2 for at in wrapped(y, 4)]
-    at_core = wrapped(slab - z * 8 - y * 2, 2)
 
     def block_of(owner):
         return pl.ds(pl.multiple_of(owner * BLOCK, BLOCK), BLOCK)

time: 29 us -> 29 us (level)
  no operation moved by 1% of the time
where the time goes in v7:
time: 29 us; the launch traced here: 28.9 us
  Pallas kernels  28.9 us (100%)
    pallas_call x1, Pallas kernels, exchange(): pl.pallas_call(exchange_kernel, in_specs=[pl.BlockSpec(memory_space=pl.AN...  24.8 us
    pallas_call x1, Pallas kernels, inverse(): pl.pallas_call(inverse_kernel, in_specs=[pl.BlockSpec(memory_space=pltpu....  4.1 us

profile of v7, /device:TPU:1, one launch (start us, length us, event | category | flops | bytes accessed | tf_op | source)
XLA Modules:
  0.0 28.9 jit_solution(15686638053693542523)
XLA Ops:
  0.0 24.8 %shard_map.73 = (f32[2,256,128]{2,1,0:T(8,128)S(1)}, f32[2,64,32,512]{3,2,1,0:T(8,128)S(1)}, bf16[256,512]{1,0:T(8,128)(2,1)S(1)}) custom-call(bf16[2,64,32,512]{3,2,1,0:T(8,128)(2,1)} %field_ref.1, f32[2,16,256,128]{3,2,1,0:T(8,128)} %bitcast.2, bf16[512,256]{1,0:T(8,128)(2,1)} %constant.8.clone.zt_hbm, f32[16,128]{1,0:T(8,128)} %constant.9.clone.x_forward_hbm, ...), custom_call_target="tpu_custom_call" | custom-call | tf_op jit(solution)/shard_map/pallas_call | solution.py:490
  24.8 4.1 %shard_map.74 = f32[2,64,32,512]{3,2,1,0:T(8,128)} custom-call(f32[2,256,128]{2,1,0:T(8,128)S(1)} %get-tuple-element.8.modes_ref, f32[2,64,32,512]{3,2,1,0:T(8,128)S(1)} %get-tuple-element.9.field_ref, bf16[256,512]{1,0:T(8,128)(2,1)S(1)} %get-tuple-element.10.table_ref), custom_call_target="tpu_custom_call" | custom-call | tf_op jit(solution)/shard_map/pallas_call | solution.py:635
